TPU v7x, 128 devices: a whole 4x4x4 slice. The times are simulated.
128 devices in a mesh: group: 4 (over x), brick: 32 (over y, z, core).
Axes of the slice: x: 4, y: 4, z: 4, core: 2. Of those that a mesh axis runs over, the one named last changes fastest.
Arguments:
- forcing_vector: float32 [1024, 64, 256], P(('group', 'brick')), may hold values from -6 to 6
- thermal_iterate: float32 [1024, 64, 256], P(('group', 'brick')), may hold values from -6 to 6
- storage_over_step: float32 [1024, 64, 256], P(('group', 'brick')), may hold values from 0.05 to 1
- opening_shares: float32 [3, 1024, 64, 256], P(None, ('group', 'brick')), may hold values from 0.05 to 1
- flow_speed: float32 [3, 1024, 64, 256], P(None, ('group', 'brick')), may hold values from 0 to 1
- diffusivity_root: float32 [1024, 64, 256], P(('group', 'brick')), may hold values from 0.5 to 2
- sanction_weight: float32 [1024, 64, 256], P(('group', 'brick')), may hold values from 0.5 to 4
- rigidity_matrix: float32 [3, 8, 8], replicated, may hold values from -0.3 to 3.4, as said below
- contact_fluid_part: int32 [128, 128], P('brick'), may hold values from 0 to 2
- contact_fluid_volume: int32 [128, 128], P('brick'), may hold values from 0 to 131071
- contact_solid_vertex: int32 [128, 128], P('brick'), may hold values from 0 to 131071
- exchange_rate_factor: float32 [128, 128], P('brick'), may hold values from 0.5 to 4
Outputs:
- updated: float32 [1024, 64, 256], P(('group', 'brick'))
Inputs may be any that keep to these rules, and one draw needn't show every extreme that they name: `rigidity_matrix`: symmetric along the last two dimensions, each diagonal entry larger than the sum of magnitudes of the other entries of its row.
All inputs are finite; a program needn't handle non-finite values.
Results may differ from a plain program's by a relative error of at most 0.0003.
Values sent between devices are 32-bit elements; how exact they have to be, the bound alone decides.
A program may use at most 128 MiB of HBM per device.

v0:
```python
import jax
import jax.numpy as jnp
from jax import lax
from jax.sharding import PartitionSpec as P

ITERS = 8


HIGH = lax.Precision.HIGHEST


def passed_along(value, axis, steps):
    count = lax.axis_size(axis)
    leading, last = (max(0, -steps), min(count, count - steps))
    return lax.ppermute(value, axis, [(source, source + steps) for source in range(leading, last)])


def extended(cells, sides, width):
    for axis, dim in sides:
        count = lax.axis_size(axis)
        ends = count - 1
        head = lax.slice_in_dim(cells, 0, width, axis=dim)
        tail = lax.slice_in_dim(cells, cells.shape[dim] - width, cells.shape[dim], axis=dim)
        cells = jnp.concatenate(
            [
                lax.ppermute(tail, axis, [(i, (i + 1) % count) for i in range(ends)]),
                cells,
                lax.ppermute(head, axis, [((i + 1) % count, i) for i in range(ends)]),
            ],
            axis=dim,
        )
    return cells


def shift_next(v, axis):
    size = v.shape[axis]
    inner = lax.slice_in_dim(v, 1, size, axis=axis)
    zero = jnp.zeros_like(lax.slice_in_dim(v, 0, 1, axis=axis))
    return jnp.concatenate([inner, zero], axis=axis)


def shift_prev(v, axis):
    size = v.shape[axis]
    inner = lax.slice_in_dim(v, 0, size - 1, axis=axis)
    zero = jnp.zeros_like(lax.slice_in_dim(v, 0, 1, axis=axis))
    return jnp.concatenate([zero, inner], axis=axis)


def open_faces(shape, axis):
    index = lax.broadcasted_iota(jnp.int32, shape, axis)
    return (index < shape[axis] - 1).astype(jnp.float32)


def element_faces(shape, axis, nodes):
    index = lax.broadcasted_iota(jnp.int32, shape, axis)
    inside = (index % nodes == nodes - 1) & (index < shape[axis] - 1)
    return inside.astype(jnp.float32)


def stiffness_apply(u, rigidity_matrix):
    nodes = rigidity_matrix.shape[1]
    rows, width, depth = u.shape
    block = min(depth, 128)
    along_x = jnp.einsum("pq,qyz->pyz", rigidity_matrix[0], u, precision=HIGH)
    split_y = u.reshape(rows, width // nodes, nodes, depth)
    along_y = jnp.einsum("pq,xeqz->xepz", rigidity_matrix[1], split_y, precision=HIGH).reshape(
        rows, width, depth
    )
    wide = jnp.kron(jnp.eye(block // nodes, dtype=jnp.float32), rigidity_matrix[2])
    split_z = u.reshape(rows, width, depth // block, block)
    along_z = jnp.einsum("xyeq,pq->xyep", split_z, wide, precision=HIGH).reshape(rows, width, depth)
    return along_x + along_y + along_z


def least_squares(hess, beta):
    gram = jnp.dot(hess.T, hess, precision=HIGH)
    lower = jnp.linalg.cholesky(gram)
    right = (beta * hess[0])[:, None]
    middle = lax.linalg.triangular_solve(lower, right, left_side=True, lower=True)
    coeffs = lax.linalg.triangular_solve(
        lower, middle, left_side=True, lower=True, transpose_a=True
    )
    return coeffs[:, 0]


def shards(
    forcing_vector,
    thermal_iterate,
    storage_over_step,
    opening_shares,
    flow_speed,
    diffusivity_root,
    sanction_weight,
    rigidity_matrix,
    contact_fluid_part,
    contact_fluid_volume,
    contact_solid_vertex,
    exchange_rate_factor,
):
    groups = lax.axis_size("group")
    bricks = lax.axis_size("brick")
    group_id = lax.axis_index("group")
    brick_id = lax.axis_index("brick")
    solid = group_id == groups - 1
    solid_flag = solid.astype(jnp.float32)
    fluid_flag = 1.0 - solid_flag
    rows, width, depth = forcing_vector.shape
    nodes = rigidity_matrix.shape[1]
    device = group_id * bricks + brick_id
    first_solid = (groups - 1) * bricks
    unrolled_array = thermal_iterate.reshape(-1)
    owned = (contact_fluid_part == group_id).astype(jnp.float32)
    target = jnp.where(solid, contact_solid_vertex, contact_fluid_volume).reshape(-1)
    picked = unrolled_array[target].reshape(contact_solid_vertex.shape)
    wall, near = lax.psum((picked * solid_flag, picked * owned * fluid_flag), "group")
    extra_rhs = jnp.where(
        solid, exchange_rate_factor * (near - wall), exchange_rate_factor * wall * owned
    )
    extra_diag = exchange_rate_factor * owned * fluid_flag
    rhs = (
        forcing_vector.reshape(-1)
        .at[target]
        .add(extra_rhs.reshape(-1))
        .reshape(forcing_vector.shape)
    )
    fluid_diag = (
        storage_over_step.reshape(-1)
        .at[target]
        .add(extra_diag.reshape(-1))
        .reshape(forcing_vector.shape)
    )
    shape = (rows, width, depth)
    global_row = device * rows + lax.broadcasted_iota(jnp.int32, shape, 0)
    face_x = opening_shares[0] * (global_row != first_solid * rows - 1).astype(jnp.float32)
    face_y = opening_shares[1] * open_faces(shape, 1)
    face_z = opening_shares[2] * open_faces(shape, 2)
    rims = passed_along(
        jnp.stack([face_x[-1], flow_speed[0][-1], sanction_weight[-1]]), ("group", "brick"), 1
    )
    face_low = rims[0]
    speed_low = rims[1]
    weight_low = rims[2]
    pair_low = 0.5 * (weight_low + sanction_weight[0]) * (device != first_solid).astype(jnp.float32)
    pair_up = passed_along(pair_low, "brick", -1)
    pair_y = (
        0.5 * (sanction_weight + shift_next(sanction_weight, 1)) * element_faces(shape, 1, nodes)
    )
    pair_z = (
        0.5 * (sanction_weight + shift_next(sanction_weight, 2)) * element_faces(shape, 2, nodes)
    )
    local_square = jnp.sum(rhs * rhs)
    solution = jnp.zeros_like(rhs)
    resid = rhs
    columns = []
    fluid_square, solid_square = lax.psum(
        (local_square * fluid_flag, local_square * solid_flag), ("group", "brick")
    )
    beta = jnp.sqrt(fluid_square)
    basis = [rhs / beta]
    direction = rhs
    norm_now = solid_square
    for step in range(ITERS):
        vector = jnp.where(solid, direction, basis[step])
        padded = extended(vector, ((("group", "brick"), 0),), 1)
        below = padded[0]
        above = padded[-1]

        def fluid_branch(unused):
            following = jnp.concatenate([vector[1:], above[None]], axis=0)
            flux_x = face_x * ((1.0 + flow_speed[0]) * vector - following)
            flux_low = face_low * ((1.0 + speed_low) * below - vector[0])
            out = (
                fluid_diag * vector
                + flux_x
                - jnp.concatenate([flux_low[None], flux_x[:-1]], axis=0)
            )
            flux_y = face_y * ((1.0 + flow_speed[1]) * vector - shift_next(vector, 1))
            flux_z = face_z * ((1.0 + flow_speed[2]) * vector - shift_next(vector, 2))
            return out + flux_y - shift_prev(flux_y, 1) + flux_z - shift_prev(flux_z, 2)

        def solid_branch(unused):
            out = storage_over_step * vector + diffusivity_root * stiffness_apply(
                diffusivity_root * vector, rigidity_matrix
            )
            jump_up = pair_up * (vector[-1] - above)
            jump_low = pair_low * (below - vector[0])
            out = out.at[0].add(-jump_low).at[rows - 1].add(jump_up)
            jump_y = pair_y * (vector - shift_next(vector, 1))
            jump_z = pair_z * (vector - shift_next(vector, 2))
            return out + jump_y - shift_prev(jump_y, 1) + jump_z - shift_prev(jump_z, 2)

        image = lax.cond(solid, solid_branch, fluid_branch, 0)
        inner = jnp.stack([jnp.sum(basis[j] * image) for j in range(step + 1)])
        heights, curvature = lax.psum(
            (inner * fluid_flag, jnp.sum(direction * image) * solid_flag), ("group", "brick")
        )
        fresh = image
        for j in range(step + 1):
            fresh = fresh - heights[j] * basis[j]
        alpha = norm_now / curvature
        solution = solution + alpha * direction
        resid = resid - alpha * image
        fresh_square, norm_next = lax.psum(
            (jnp.sum(fresh * fresh) * fluid_flag, jnp.sum(resid * resid) * solid_flag),
            ("group", "brick"),
        )
        length = jnp.sqrt(fresh_square)
        basis.append(fresh / length)
        columns.append(
            jnp.concatenate([heights, length[None], jnp.zeros((ITERS - 1 - step,), jnp.float32)])
        )
        direction = resid + norm_next / norm_now * direction
        norm_now = norm_next
    coeffs = least_squares(jnp.stack(columns, axis=1), beta)
    fluid_new = jnp.zeros_like(rhs)
    for step in range(ITERS):
        fluid_new = fluid_new + coeffs[step] * basis[step]
    return jnp.where(solid, solution, fluid_new)


def solution(mesh):
    return jax.shard_map(
        shards,
        mesh=mesh,
        in_specs=(
            P(("group", "brick"), None, None),
            P(("group", "brick"), None, None),
            P(("group", "brick"), None, None),
            P(None, ("group", "brick"), None, None),
            P(None, ("group", "brick"), None, None),
            P(("group", "brick"), None, None),
            P(("group", "brick"), None, None),
            P(),
            P("brick", None),
            P("brick", None),
            P("brick", None),
            P("brick", None),
        ),
        out_specs=P(("group", "brick"), None, None),
        check_vma=False,
    )
```

profile of v0, /device:TPU:0, one launch (start us, length us, event | category | flops | bytes accessed | tf_op | source)
XLA Modules:
  0.0 1639.6 jit_solution(3952403105590713106)
XLA Ops:
  6.6 10.6 all-reduce.80
  22.3 66.5 %psum.248 = f32[]{:T(128)} all-reduce(f32[]{:T(128)S(6)} %mul.1371), channel_id=1, replica_groups=mesh['group'=4,'brick'=32] {'group','brick'}, use_global_device_ids=true, to_apply=%region_5.6 | all-reduce | flops 1 | bytes 8 | tf_op jit(solution)/shard_map/psum | solution.py:155
  128.0 5.7 conditional.8
  135.8 89.1 %all-reduce.79 = (f32[]{:T(128)}, f32[]{:T(128)}, f32[1]{0:T(128)}) all-reduce(f32[]{:T(128)S(6)} %mul.1368, f32[]{:T(128)S(6)} %mul.1386, f32[1]{0:T(128)} %bitcast.162), channel_id=1, replica_groups=mesh['group'=4,'brick'=32] {'group','brick'}, use_global_device_ids=true, to_apply=%region_4.5 | all-reduce | flops 3 | bytes 24 | tf_op jit(solution)/shard_map/psum | solution.py:155
  229.0 64.5 %all-reduce.78 = (f32[]{:T(128)}, f32[]{:T(128)}) all-reduce(f32[]{:T(128)S(6)} %mul.1400, f32[]{:T(128)S(6)} %mul.1391), channel_id=1, replica_groups=mesh['group'=4,'brick'=32] {'group','brick'}, use_global_device_ids=true, to_apply=%region_16.17 | all-reduce | flops 2 | bytes 16 | tf_op jit(solution)/shard_map/psum | solution.py:203
  302.7 4.8 conditional.9
  311.3 84.1 %all-reduce.77 = (f32[]{:T(128)}, f32[2]{0:T(128)S(1)}) all-reduce(f32[]{:T(128)S(6)} %mul.1402, f32[2]{0:T(128)S(1)} %maximum_multiply_fusion), channel_id=1, replica_groups=mesh['group'=4,'brick'=32] {'group','brick'}, use_global_device_ids=true, to_apply=%region_20.21 | all-reduce | flops 3 | bytes 24 | tf_op jit(solution)/shard_map/psum | solution.py:194
  401.6 64.6 %all-reduce.76 = (f32[]{:T(128)}, f32[]{:T(128)}) all-reduce(f32[]{:T(128)S(6)} %mul.1407, f32[]{:T(128)S(6)} %mul.1419), channel_id=1, replica_groups=mesh['group'=4,'brick'=32] {'group','brick'}, use_global_device_ids=true, to_apply=%region_22.23 | all-reduce | flops 2 | bytes 16 | tf_op jit(solution)/shard_map/psum | solution.py:203
  474.9 4.8 conditional.10
  484.5 87.0 %all-reduce.75 = (f32[]{:T(128)}, f32[3]{0:T(128)S(1)}) all-reduce(f32[]{:T(128)S(6)} %mul.1421, f32[3]{0:T(128)S(1)} %maximum_multiply_fusion.1), channel_id=1, replica_groups=mesh['group'=4,'brick'=32] {'group','brick'}, use_global_device_ids=true, to_apply=%region_31.32 | all-reduce | flops 4 | bytes 32 | tf_op jit(solution)/shard_map/psum | solution.py:194
  579.4 64.5 %all-reduce.74 = (f32[]{:T(128)}, f32[]{:T(128)}) all-reduce(f32[]{:T(128)S(6)} %mul.1426, f32[]{:T(128)S(6)} %mul.1441), channel_id=1, replica_groups=mesh['group'=4,'brick'=32] {'group','brick'}, use_global_device_ids=true, to_apply=%region_33.34 | all-reduce | flops 2 | bytes 16 | tf_op jit(solution)/shard_map/psum | solution.py:203
  662.5 86.5 %all-reduce.73 = (f32[]{:T(128)}, f32[4]{0:T(128)S(1)}) all-reduce(f32[]{:T(128)S(6)} %mul.1443, f32[4]{0:T(128)S(1)} %maximum_multiply_fusion.2), channel_id=1, replica_groups=mesh['group'=4,'brick'=32] {'group','brick'}, use_global_device_ids=true, to_apply=%region_43.44 | all-reduce | flops 5 | bytes 40 | tf_op jit(solution)/shard_map/psum | solution.py:194
  750.9 5.4 multiply_reduce_fusion.42
  757.6 64.6 %all-reduce.72 = (f32[]{:T(128)}, f32[]{:T(128)}) all-reduce(f32[]{:T(128)S(6)} %mul.1448, f32[]{:T(128)S(6)} %mul.1466), channel_id=1, replica_groups=mesh['group'=4,'brick'=32] {'group','brick'}, use_global_device_ids=true, to_apply=%region_45.46 | all-reduce | flops 2 | bytes 16 | tf_op jit(solution)/shard_map/psum | solution.py:203
  830.9 5.5 conditional.12
  842.5 87.0 %all-reduce.71 = (f32[]{:T(128)}, f32[5]{0:T(128)S(1)}) all-reduce(f32[]{:T(128)S(6)} %mul.1468, f32[5]{0:T(128)S(1)} %broadcast_multiply_fusion.11), channel_id=1, replica_groups=mesh['group'=4,'brick'=32] {'group','brick'}, use_global_device_ids=true, to_apply=%region_56.57 | all-reduce | flops 6 | bytes 48 | tf_op jit(solution)/shard_map/psum | solution.py:194
  931.4 6.4 multiply_reduce_fusion.35
  939.2 64.5 %all-reduce.70 = (f32[]{:T(128)}, f32[]{:T(128)}) all-reduce(f32[]{:T(128)S(6)} %mul.1473, f32[]{:T(128)S(6)} %mul.1494), channel_id=1, replica_groups=mesh['group'=4,'brick'=32] {'group','brick'}, use_global_device_ids=true, to_apply=%region_58.59 | all-reduce | flops 2 | bytes 16 | tf_op jit(solution)/shard_map/psum | solution.py:203
  1012.7 5.3 conditional.13
  1026.4 86.5 %all-reduce.69 = (f32[]{:T(128)}, f32[6]{0:T(128)S(1)}) all-reduce(f32[]{:T(128)S(6)} %mul.1496, f32[6]{0:T(128)S(1)} %broadcast_multiply_fusion.10), channel_id=1, replica_groups=mesh['group'=4,'brick'=32] {'group','brick'}, use_global_device_ids=true, to_apply=%region_70.71 | all-reduce | flops 7 | bytes 56 | tf_op jit(solution)/shard_map/psum | solution.py:194
  1118.6 6.9 multiply_reduce_fusion.20
  1126.8 64.5 %all-reduce.68 = (f32[]{:T(128)}, f32[]{:T(128)}) all-reduce(f32[]{:T(128)S(6)} %mul.1501, f32[]{:T(128)S(6)} %mul.1525), channel_id=1, replica_groups=mesh['group'=4,'brick'=32] {'group','brick'}, use_global_device_ids=true, to_apply=%region_72.73 | all-reduce | flops 2 | bytes 16 | tf_op jit(solution)/shard_map/psum | solution.py:203
  1200.4 5.5 conditional.14
  1209.2 86.7 %psum.273 = f32[]{:T(128)} all-reduce(f32[]{:T(128)S(6)} %mul.1527), channel_id=1, replica_groups=mesh['group'=4,'brick'=32] {'group','brick'}, use_global_device_ids=true, to_apply=%region_85.86 | all-reduce | flops 1 | bytes 8 | tf_op jit(solution)/shard_map/psum | solution.py:194
  1305.3 64.6 %psum.275 = f32[7]{0:T(128)S(1)} all-reduce(f32[7]{0:T(128)S(1)} %broadcast_multiply_fusion.9), channel_id=1, replica_groups=mesh['group'=4,'brick'=32] {'group','brick'}, use_global_device_ids=true, to_apply=%region_95.96 | all-reduce | flops 7 | bytes 56 | tf_op jit(solution)/shard_map/psum | solution.py:194
  1370.6 7.7 multiply_reduce_fusion.10
  1379.4 62.0 %all-reduce.67 = (f32[]{:T(128)}, f32[]{:T(128)}) all-reduce(f32[]{:T(128)S(6)} %mul.1532, f32[]{:T(128)S(6)} %mul.1559), channel_id=1, replica_groups=mesh['group'=4,'brick'=32] {'group','brick'}, use_global_device_ids=true, to_apply=%region_87.88 | all-reduce | flops 2 | bytes 16 | tf_op jit(solution)/shard_map/psum | solution.py:203
  1460.9 5.0 stack.206
  1466.4 85.9 %psum.278 = f32[8]{0:T(128)S(1)} all-reduce(f32[8]{0:T(128)S(1)} %broadcast_multiply_fusion.8), channel_id=1, replica_groups=mesh['group'=4,'brick'=32] {'group','brick'}, use_global_device_ids=true, to_apply=%region_110.111 | all-reduce | flops 8 | bytes 64 | tf_op jit(solution)/shard_map/psum | solution.py:194
  1553.1 7.3 multiply_reduce_fusion
  1561.1 62.9 %all-reduce.66 = (f32[]{:T(128)}, f32[]{:T(128)}) all-reduce(f32[]{:T(128)S(6)} %mul.1591, f32[]{:T(128)S(6)} %mul.1561), channel_id=1, replica_groups=mesh['group'=4,'brick'=32] {'group','brick'}, use_global_device_ids=true, to_apply=%region_112.113 | all-reduce | flops 2 | bytes 16 | tf_op jit(solution)/shard_map/psum | solution.py:203
  1630.1 9.0 add_select_fusion
  (348 shorter events, 208.6 us)
Async XLA Ops:
  20.7 72.2 %copy-start.1 = (f32[3,8,64,256]{3,2,1,0:T(8,128)S(1)}, f32[3,8,64,256]{3,2,1,0:T(8,128)}, u32[]{:S(2)}) copy-start(f32[3,8,64,256]{3,2,1,0:T(8,128)} %param.64) | copy-start | bytes 4718596
  90.2 35.7 %collective-permute-start.2 = (f32[1,64,256]{2,1,0:T(8,128)}, f32[1,64,256]{2,1,0:T(8,128)S(1)}, u32[]{:S(2)}, u32[]{:S(2)}) collective-permute-start(f32[1,64,256]{2,1,0:T(8,128)} %get-tuple-element.1241), channel_id=1, source_target_pairs={{0,1},{1,2},{2,3},{3,4},{4,5},{5,6},{6,7},{7,8},{8,9},{9,10},{10,1... | collective-permute-start | bytes 196616 | tf_op jit(solution)/shard_map/ppermute | solution.py:26
  91.6 34.4 %collective-permute-start = (f32[1,64,256]{2,1,0:T(8,128)}, f32[1,64,256]{2,1,0:T(8,128)}, u32[]{:S(2)}, u32[]{:S(2)}) collective-permute-start(f32[1,64,256]{2,1,0:T(8,128)} %get-tuple-element.1242), channel_id=1, source_target_pairs={{1,0},{2,1},{3,2},{4,3},{5,4},{6,5},{7,6},{8,7},{9,8},{10,9},{11,1... | collective-permute-start | bytes 196616 | tf_op jit(solution)/shard_map/ppermute | solution.py:28
  96.8 31.2 %copy-start.8 = (f32[8,64,256]{2,0,1:T(8,128)}, f32[8,64,256]{2,0,1:T(8,128)S(1)}, u32[]{:S(2)}) copy-start(f32[8,64,256]{2,0,1:T(8,128)S(1)} %fusion.282) | copy-start | bytes 1572868
  97.0 25.8 %collective-permute-start.1 = (f32[3,64,256]{2,0,1:T(4,128)S(1)}, f32[3,64,256]{2,0,1:T(4,128)}, u32[]{:S(2)}, u32[]{:S(2)}) collective-permute-start(f32[3,64,256]{2,0,1:T(4,128)S(1)} %pad_maximum_fusion), channel_id=1, source_target_pairs={{0,1},{1,2},{2,3},{3,4},{4,5},{5,6},{6,7},{7,8},{8,9},{9,10},{10,1... | collective-permute-start | bytes 589832 | tf_op jit(solution)/shard_map/ppermute | solution.py:15
  124.6 3.3 collective-permute-start.3
  133.7 161.1 %copy-start.67 = (f32[8,64,256]{2,1,0:T(8,128)}, f32[8,64,256]{2,1,0:T(8,128)S(1)}, u32[]{:S(2)}) copy-start(f32[8,64,256]{2,1,0:T(8,128)S(1)} %get-tuple-element.1029) | copy-start | bytes 1572868
  298.2 2.6 collective-permute-start.5
  299.5 3.1 collective-permute-start.4
  307.5 89.8 %copy-start.68 = (f32[8,64,256]{2,1,0:T(8,128)S(1)}, f32[8,64,256]{2,1,0:T(8,128)}, u32[]{:S(2)}) copy-start(f32[8,64,256]{2,1,0:T(8,128)} %copy-done.67) | copy-start | bytes 1572868
  400.3 74.7 %copy-start.9 = (f32[8,64,256]{2,0,1:T(8,128)S(1)}, f32[8,64,256]{2,0,1:T(8,128)}, u32[]{:S(2)}) copy-start(f32[8,64,256]{2,0,1:T(8,128)} %copy-done.8) | copy-start | bytes 1572868
  400.3 74.7 %copy-start.16 = (f32[8,64,256]{2,1,0:T(8,128)S(1)}, f32[8,64,256]{2,1,0:T(8,128)}, u32[]{:S(2)}) copy-start(f32[8,64,256]{2,1,0:T(8,128)} %reshape.915) | copy-start | bytes 1572868
  470.5 2.6 collective-permute-start.7
  471.8 3.1 collective-permute-start.6
  479.8 93.6 %copy-start.70 = (f32[8,64,256]{2,1,0:T(8,128)}, f32[8,64,256]{2,1,0:T(8,128)S(1)}, u32[]{:S(2)}) copy-start(f32[8,64,256]{2,1,0:T(8,128)S(1)} %get-tuple-element.1031) | copy-start | bytes 1572868
  648.2 2.6 collective-permute-start.9
  649.5 3.1 collective-permute-start.8
  826.4 2.6 collective-permute-start.11
  827.7 3.1 collective-permute-start.10
  1008.3 2.6 collective-permute-start.13
  1009.6 3.1 collective-permute-start.12
  1196.0 3.9 collective-permute-start.15
  1197.3 3.1 collective-permute-start.14
  1446.3 3.7 collective-permute-start.17
  1448.2 4.2 collective-permute-start.16
  1458.0 95.1 %copy-start.39 = (f32[8,64,256]{2,1,0:T(8,128)S(1)}, f32[8,64,256]{2,1,0:T(8,128)}, u32[]{:S(2)}) copy-start(f32[8,64,256]{2,1,0:T(8,128)} %get-tuple-element.1224) | copy-start | bytes 1572868
  1553.1 71.7 %copy-start.120 = (f32[9,1]{0,1:T(1,128)S(1)}, f32[9,1]{0,1:T(1,128)}, u32[]{:S(2)}) copy-start(f32[9,1]{0,1:T(1,128)} %maximum_bitcast_fusion) | copy-start | bytes 112
  1553.1 71.7 %copy-start.121 = (f32[9,1]{0,1:T(1,128)S(1)}, f32[9,1]{0,1:T(1,128)}, u32[]{:S(2)}) copy-start(f32[9,1]{0,1:T(1,128)} %maximum_bitcast_fusion.1) | copy-start | bytes 112
  1553.1 71.7 %copy-start.122 = (f32[9,1]{0,1:T(1,128)S(1)}, f32[9,1]{0,1:T(1,128)}, u32[]{:S(2)}) copy-start(f32[9,1]{0,1:T(1,128)} %maximum_bitcast_fusion.2) | copy-start | bytes 112
  1553.1 71.7 %copy-start.123 = (f32[9,1]{0,1:T(1,128)S(1)}, f32[9,1]{0,1:T(1,128)}, u32[]{:S(2)}) copy-start(f32[9,1]{0,1:T(1,128)} %maximum_bitcast_fusion.3) | copy-start | bytes 112
  1553.1 71.7 %copy-start.124 = (f32[9,1]{0,1:T(1,128)S(1)}, f32[9,1]{0,1:T(1,128)}, u32[]{:S(2)}) copy-start(f32[9,1]{0,1:T(1,128)} %maximum_bitcast_fusion.4) | copy-start | bytes 112
  1553.1 71.7 %copy-start.125 = (f32[9,1]{0,1:T(1,128)S(1)}, f32[9,1]{0,1:T(1,128)}, u32[]{:S(2)}) copy-start(f32[9,1]{0,1:T(1,128)} %maximum_bitcast_fusion.5) | copy-start | bytes 112
  (37 other events, 243.3 us)
where the time goes:
time: 1650 us; the launch traced here: 1640 us
  blocking collectives  1350 us (82%)
  other arithmetic  147 us (9%)
  local copies, waits for them, and re-layouts  58.8 us (4%)
  between operations  44.2 us (3%)
  starting transfers between devices  26.5 us (2%)
    psum x8, blocking collectives, shards(): lax.psum((inner * fluid_flag, jnp.sum(direction * image) * solid_flag), (...  668 us
    psum x8, blocking collectives, shards(): lax.psum((jnp.sum(fresh * fresh) * fluid_flag, jnp.sum(resid * resid) * s...  512 us
    psum x2, blocking collectives, shards(): lax.psum((local_square * fluid_flag, local_square * solid_flag), ('group'...  156 us
  transfers between devices with their start and end apart: 18, of which 8 were waited for; matrix products, arithmetic and copies ran while one was open for 2% of the time, Pallas kernels for 0%

commit v1 on v0

--- a/solution.py
+++ b/solution.py
@@ -1,6 +1,10 @@
+import functools
+
 import jax
 import jax.numpy as jnp
 from jax import lax
+from jax.experimental import pallas as pl
+from jax.experimental.pallas import tpu as pltpu
 from jax.sharding import PartitionSpec as P
 
 ITERS = 8
@@ -83,7 +87,7 @@
     return coeffs[:, 0]
 
 
-def shards(
+def iterated(
     forcing_vector,
     thermal_iterate,
     storage_over_step,
@@ -218,6 +222,794 @@
     return jnp.where(solid, solution, fluid_new)
 
 
+F32 = jnp.float32
+BF16 = jnp.bfloat16
+MESH = pl.DeviceIdType.MESH
+PIVOT_LEAST = 1e-3
+REFINE_MOST = 3e-4
+
+
+def iota(shape, dim):
+    return lax.broadcasted_iota(jnp.int32, shape, dim)
+
+
+def pieces(x):
+    high = x.astype(BF16)
+    return high, (x - high.astype(F32)).astype(BF16)
+
+
+def total(x):
+    return jnp.sum(jnp.sum(x, axis=0, keepdims=True), axis=1, keepdims=True)
+
+
+def greatest(x):
+    return jnp.max(jnp.max(x, axis=0, keepdims=True), axis=1, keepdims=True)
+
+
+def dot(a, b, dims):
+    return lax.dot_general(a, b, ((dims[0], dims[1]), ((), ())), preferred_element_type=F32)
+
+
+def shift_rows(x, gamma):
+    size = x.shape[0]
+    after = pltpu.roll(x, size - 1, 0)
+    row = iota(x.shape, 0)
+    out = gamma * x + 0.5 * (pltpu.roll(x, 1, 0) + after) + jnp.where(row == 0, 0.5 * after, 0.0)
+    return jnp.where(row < ITERS, out, 0.0)
+
+
+def shift_lanes(x, gamma):
+    size = x.shape[1]
+    after = pltpu.roll(x, size - 1, 1)
+    lane = iota(x.shape, 1)
+    out = gamma * x + 0.5 * (pltpu.roll(x, 1, 1) + after) + jnp.where(lane == 0, 0.5 * after, 0.0)
+    return jnp.where(lane < ITERS, out, 0.0)
+
+
+def projected(gram, gamma, fluid):
+    shape = gram.shape
+    row, lane = iota(shape, 0), iota(shape, 1)
+    wide = shift_lanes(gram, gamma)
+    if fluid:
+        normal, right = shift_rows(wide, gamma), shift_rows(gram, gamma)
+    else:
+        normal, right = jnp.where(row < ITERS, wide, 0.0), jnp.where(row < ITERS, gram, 0.0)
+    table = jnp.where(lane < ITERS, normal, 0.0)
+    table = jnp.where((lane == row + 8) & (row < ITERS), 1.0, table)
+    table = jnp.where(lane == 16, pltpu.roll(right, 16, 1), table)
+    margin = None
+    for k in range(ITERS):
+        pivot = table[k : k + 1, k : k + 1]
+        spare = pivot - PIVOT_LEAST * normal[k : k + 1, k : k + 1]
+        margin = spare if margin is None else jnp.minimum(margin, spare)
+        scaled = table[k : k + 1, :] * (1.0 / pivot)
+        column = jnp.where(row[:, :1] == k, 0.0, table[:, k : k + 1])
+        table = jnp.where(row == k, scaled, table - column * scaled)
+    coeffs = jnp.broadcast_to(table[:, 16:17], shape)
+    inverse = jnp.where(lane < ITERS, pltpu.roll(table, shape[1] - 8, 1), 0.0)
+    applied = gamma * coeffs + 0.5 * (pltpu.roll(coeffs, 1, 0) + pltpu.roll(coeffs, shape[0] - 1, 0))
+    applied = applied + jnp.where(row == 1, 0.5 * pltpu.roll(coeffs, 1, 0), 0.0)
+    rest = jnp.where(row == 0, 1.0, 0.0) - applied
+    image = jnp.broadcast_to(jnp.sum(gram * rest, axis=0, keepdims=True), shape)
+    image = shift_lanes(image, gamma) if fluid else jnp.where(lane < ITERS, image, 0.0)
+    change = jnp.sum(inverse * image, axis=1, keepdims=True)
+    coeffs = coeffs[:, :1] + change
+    size = jnp.sum(jnp.abs(coeffs), axis=0, keepdims=True)
+    moved = jnp.sum(jnp.abs(change), axis=0, keepdims=True)
+    good = (margin > 0.0) & (moved < REFINE_MOST * size)
+    return coeffs, jnp.where(good, 1.0, 0.0)
+
+
+def kernel(
+    groups,
+    bricks,
+    forcing_hbm,
+    thermal_hbm,
+    storage_hbm,
+    opening_hbm,
+    flow_hbm,
+    root_hbm,
+    weight_hbm,
+    rigidity_hbm,
+    part_hbm,
+    volume_hbm,
+    vertex_hbm,
+    factor_hbm,
+    out_hbm,
+    flag_hbm,
+    thermal,
+    forcing,
+    storage,
+    opening,
+    flow,
+    root,
+    weight,
+    rigidity,
+    part,
+    volume,
+    vertex,
+    factor,
+    basis,
+    ax,
+    gx,
+    diag,
+    uy,
+    ly,
+    uz,
+    lz,
+    stiff,
+    uh,
+    ul,
+    wz,
+    wxy,
+    weight_low,
+    weight_up,
+    row_hot,
+    col_hot,
+    picked,
+    walls,
+    nears,
+    gram_tile,
+    near_slots,
+    far_slots,
+    out,
+    flag,
+    load_sem,
+    store_sem,
+    halo_send,
+    halo_recv,
+    coef_send,
+    coef_recv,
+    contact_send,
+    contact_recv,
+    near_send,
+    near_recv,
+    far_send,
+    far_recv,
+):
+    group = lax.axis_index("group")
+    brick = lax.axis_index("brick")
+    rows, width, depth = forcing.shape
+    plane = (width, depth)
+    cells = rows * width
+    solid = group == groups - 1
+    fluid = group != groups - 1
+    inner, outer = 8, bricks // 8
+    low_id = lax.rem(brick, inner)
+    high_id = group * outer + brick // inner
+    n_far = groups * outer
+    at_top = (brick == bricks - 1) & (group >= groups - 2)
+    at_bottom = (brick == 0) & ((group == 0) | (group == groups - 1))
+    has_up, has_down = jnp.logical_not(at_top), jnp.logical_not(at_bottom)
+    device = group * bricks + brick
+    up_id = lax.rem(device + 1, groups * bricks)
+    down_id = lax.rem(device + groups * bricks - 1, groups * bricks)
+    up = (up_id // bricks, lax.rem(up_id, bricks))
+    down = (down_id // bricks, lax.rem(down_id, bricks))
+
+    names = [
+        (vertex_hbm, vertex),
+        (volume_hbm, volume),
+        (thermal_hbm, thermal),
+        (part_hbm, part),
+        (factor_hbm, factor),
+        (opening_hbm, opening),
+        (flow_hbm, flow),
+        (storage_hbm, storage),
+        (weight_hbm, weight),
+        (root_hbm, root),
+        (rigidity_hbm, rigidity),
+        (forcing_hbm, forcing),
+    ]
+    loads = [pltpu.make_async_copy(s, d, load_sem.at[i]) for i, (s, d) in enumerate(names)]
+    for load in loads:
+        load.start()
+    (l_vertex, l_volume, l_thermal, l_part, l_factor, l_opening, l_flow, l_storage, l_weight, l_root, l_rigid, l_forcing) = loads
+
+    def near_peer(o):
+        peer = lax.rem(low_id + o, inner)
+        return peer, (group, (brick // inner) * inner + peer)
+
+    def far_peer(o):
+        peer = lax.rem(high_id + o, n_far)
+        return peer, (peer // outer, lax.rem(peer, outer) * inner + low_id)
+
+    barrier = pltpu.get_barrier_semaphore()
+    for o in range(1, inner):
+        pl.semaphore_signal(barrier, inc=1, device_id=near_peer(o)[1], device_id_type=MESH)
+    for o in range(1, n_far):
+        pl.semaphore_signal(barrier, inc=1, device_id=far_peer(o)[1], device_id_type=MESH)
+
+    @pl.when(has_up)
+    def _():
+        pl.semaphore_signal(barrier, inc=1, device_id=up, device_id_type=MESH)
+
+    @pl.when(has_down)
+    def _():
+        pl.semaphore_signal(barrier, inc=1, device_id=down, device_id_type=MESH)
+
+    @pl.when(at_bottom)
+    def _():
+        for k in range(ITERS):
+            basis[k, 0] = jnp.zeros(plane, F32)
+
+    @pl.when(at_top)
+    def _():
+        for k in range(ITERS):
+            basis[k, rows + 1] = jnp.zeros(plane, F32)
+
+    l_vertex.wait()
+    l_volume.wait()
+    target = jnp.where(solid, vertex[...], volume[...])
+    cell_row, cell_col = target >> 8, target & 255
+    lines = target.shape[0]
+    points = lines * 128
+    for j in range(lines):
+        span = pl.ds(j * 128, 128)
+        row_hot[:, span] = jnp.where(iota((cells, 128), 0) == cell_row[j : j + 1], 1.0, 0.0).astype(BF16)
+        col_hot[:, span] = jnp.where(iota((depth, 128), 0) == cell_col[j : j + 1], 1.0, 0.0).astype(BF16)
+    l_thermal.wait()
+    high, low = pieces(thermal[...].reshape(cells, depth))
+    hot = row_hot[...]
+    found = dot(high, hot, ((0,), (0,))) + dot(low, hot, ((0,), (0,)))
+    value = jnp.sum(found * col_hot[...].astype(F32), axis=0, keepdims=True)
+    value = jnp.concatenate([value[:, j * 128 : (j + 1) * 128] for j in range(lines)], axis=0)
+    l_part.wait()
+    l_factor.wait()
+    owned = jnp.where(part[...] == group, 1.0, 0.0)
+    picked[0:lines] = jnp.where(solid, value, value * owned)
+    picked[lines:] = jnp.zeros((8 - lines, 128), F32)
+
+    pl.semaphore_wait(barrier, inner - 1 + n_far - 1 + has_up.astype(jnp.int32) + has_down.astype(jnp.int32))
+
+    def wall_copy(g):
+        return pltpu.make_async_remote_copy(
+            picked, walls, contact_send.at[g], contact_recv.at[groups - 1], device_id=(g, brick), device_id_type=MESH
+        )
+
+    near_copy = pltpu.make_async_remote_copy(
+        picked, nears.at[group], contact_send.at[0], contact_recv.at[group], device_id=(groups - 1, brick), device_id_type=MESH
+    )
+
+    @pl.when(solid)
+    def _():
+        for g in range(groups - 1):
+            wall_copy(g).start()
+
+    @pl.when(fluid)
+    def _():
+        near_copy.start()
+
+    l_opening.wait()
+    l_flow.wait()
+    l_weight.wait()
+    coef_a = pltpu.make_async_remote_copy(
+        ax.at[rows], ax.at[0], coef_send.at[0], coef_recv.at[0], device_id=up, device_id_type=MESH
+    )
+    coef_g = pltpu.make_async_remote_copy(
+        gx.at[rows], gx.at[0], coef_send.at[1], coef_recv.at[1], device_id=up, device_id_type=MESH
+    )
+    coef_up = pltpu.make_async_remote_copy(
+        weight.at[rows - 1], weight_low, coef_send.at[0], coef_recv.at[0], device_id=up, device_id_type=MESH
+    )
+    coef_down = pltpu.make_async_remote_copy(
+        weight.at[0], weight_up, coef_send.at[1], coef_recv.at[1], device_id=down, device_id_type=MESH
+    )
+
+    @pl.when(fluid)
+    def _():
+        last = jnp.where(at_top, 0.0, opening[0, rows - 1])
+        ax[rows] = last
+        gx[rows] = last * (1.0 + flow[0, rows - 1])
+
+    @pl.when(fluid & has_up)
+    def _():
+        coef_a.start()
+        coef_g.start()
+
+    @pl.when(solid & has_up)
+    def _():
+        coef_up.start()
+
+    @pl.when(solid & has_down)
+    def _():
+        coef_down.start()
+
+    l_storage.wait()
+    l_root.wait()
+    l_rigid.wait()
+
+    def spread(values):
+        flat = jnp.concatenate([values[j : j + 1] for j in range(lines)], axis=1)
+        high, low = pieces(flat)
+        cols = col_hot[...].astype(F32)
+        return dot(row_hot[...], (cols * high.astype(F32)).astype(BF16), ((1,), (1,))) + dot(
+            row_hot[...], (cols * low.astype(F32)).astype(BF16), ((1,), (1,))
+        )
+
+    def fold(x, op):
+        y = x.reshape(width // 8, 8, depth)
+        return op(y, axis=0)
+
+    y_at, z_at = iota(plane, 0), iota(plane, 1)
+
+    def write_stats(d_max, d_min, o_sum):
+        lane = iota((8, 128), 1)
+        tile = jnp.where(lane == 0, greatest(d_max), jnp.where(lane == 1, greatest(-d_min), jnp.where(lane == 2, total(o_sum), 0.0)))
+        near_slots[0, low_id, 0:8] = tile
+
+    start = (jnp.full((8, depth), -1e30, F32), jnp.full((8, depth), 1e30, F32), jnp.zeros((8, depth), F32))
+
+    @pl.when(fluid)
+    def _():
+        extra = spread(factor[...] * owned).reshape(rows, width, depth)
+        storage[...] = storage[...] + extra
+
+        def first(r, carry):
+            a = opening[0, r]
+            ax[r + 1] = a
+            gx[r + 1] = a * (1.0 + flow[0, r])
+            return carry
+
+        lax.fori_loop(0, rows - 1, first, 0)
+
+        @pl.when(has_down)
+        def _():
+            coef_a.wait_recv()
+            coef_g.wait_recv()
+
+        @pl.when(at_bottom)
+        def _():
+            ax[0] = jnp.zeros(plane, F32)
+            gx[0] = jnp.zeros(plane, F32)
+
+        def second(r, carry):
+            d_max, d_min, o_sum = carry
+            a_y = jnp.where(y_at == width - 1, 0.0, opening[1, r])
+            g_y = a_y * (1.0 + flow[1, r])
+            g_low = pltpu.roll(g_y, 1, 0)
+            uy[r] = a_y
+            ly[r] = g_low
+            d = storage[r] + ax[r] + gx[r + 1] + g_y + pltpu.roll(a_y, 1, 0)
+            o = ax[r + 1] + gx[r] + a_y + g_low
+            a_z = jnp.where(z_at == depth - 1, 0.0, opening[2, r])
+            g_z = a_z * (1.0 + flow[2, r])
+            g_low = pltpu.roll(g_z, 1, 1)
+            uz[r] = a_z
+            lz[r] = g_low
+            d = d + g_z + pltpu.roll(a_z, 1, 1)
+            o = o + a_z + g_low
+            diag[r] = d
+            return jnp.maximum(d_max, fold(d, jnp.max)), jnp.minimum(d_min, fold(d, jnp.min)), o_sum + fold(o, jnp.sum)
+
+        write_stats(*lax.fori_loop(0, rows, second, start))
+
+    @pl.when(solid)
+    def _():
+        eye = iota((8, 8), 0) == iota((8, 8), 1)
+        both = rigidity[0] + rigidity[1] + rigidity[2]
+        size = jnp.abs(rigidity[0]) + jnp.abs(rigidity[1]) + jnp.abs(rigidity[2])
+        trace = total(jnp.where(eye, both, 0.0)) * (1.0 / 8)
+        off = total(jnp.where(eye, 0.0, size)) * (1.0 / 8)
+        block_z = jnp.where(iota((8, depth), 1) % 8 == iota((8, depth), 0), 1.0, 0.0)
+        spread_z = lax.dot_general(
+            lax.dot_general(block_z, rigidity[2], (((0,), (1,)), ((), ())), precision=HIGH, preferred_element_type=F32),
+            block_z,
+            (((1,), (0,)), ((), ())),
+            precision=HIGH,
+            preferred_element_type=F32,
+        )
+        same = (iota((depth, depth), 0) // 8) == (iota((depth, depth), 1) // 8)
+        high, low = pieces(jnp.where(same, spread_z, 0.0))
+        wz[0], wz[1] = high, low
+        outer_x = jnp.where(iota((8, 64), 1) // 8 == iota((8, 64), 0), 1.0, 0.0)
+        inner_y = jnp.where(iota((8, 64), 1) % 8 == iota((8, 64), 0), 1.0, 0.0)
+
+        def expand(matrix, hot):
+            left = lax.dot_general(hot, matrix, (((0,), (0,)), ((), ())), precision=HIGH, preferred_element_type=F32)
+            return lax.dot_general(left, hot, (((1,), (0,)), ((), ())), precision=HIGH, preferred_element_type=F32)
+
+        same_y = iota((64, 64), 0) % 8 == iota((64, 64), 1) % 8
+        same_x = iota((64, 64), 0) // 8 == iota((64, 64), 1) // 8
+        mixed = jnp.where(same_y, expand(rigidity[0], outer_x), 0.0) + jnp.where(same_x, expand(rigidity[1], inner_y), 0.0)
+        high, low = pieces(mixed)
+        wxy[...] = jnp.concatenate([high, high, low], axis=1)
+
+        @pl.when(has_down)
+        def _():
+            coef_up.wait_recv()
+            gx[0] = 0.5 * (weight_low[...] + weight[0])
+
+        @pl.when(at_bottom)
+        def _():
+            gx[0] = jnp.zeros(plane, F32)
+
+        @pl.when(has_up)
+        def _():
+            coef_down.wait_recv()
+            ax[rows] = 0.5 * (weight[rows - 1] + weight_up[...])
+
+        @pl.when(at_top)
+        def _():
+            ax[rows] = jnp.zeros(plane, F32)
+
+        def second(r, carry):
+            d_max, d_min, o_sum = carry
+            w = weight[r]
+            b_y = jnp.where((y_at % 8 == 7) & (y_at < width - 1), 0.5 * (w + pltpu.roll(w, width - 1, 0)), 0.0)
+            b_low = pltpu.roll(b_y, 1, 0)
+            uy[r] = b_y
+            ly[r] = b_low
+            pair = b_y + b_low
+            b_z = jnp.where((z_at % 8 == 7) & (z_at < depth - 1), 0.5 * (w + pltpu.roll(w, depth - 1, 1)), 0.0)
+            b_low = pltpu.roll(b_z, 1, 1)
+            uz[r] = b_z
+            lz[r] = b_low
+            pair = pair + b_z + b_low
+            d = storage[r] + pair
+            diag[r] = d
+            square = root[r] * root[r]
+            whole = d + square * trace
+            o = pair + square * off
+            return jnp.maximum(d_max, fold(whole, jnp.max)), jnp.minimum(d_min, fold(whole, jnp.min)), o_sum + fold(o, jnp.sum)
+
+        write_stats(*lax.fori_loop(0, rows, second, start))
+        diag[0] = diag[0] + gx[0]
+        diag[rows - 1] = diag[rows - 1] + ax[rows]
+
+    def near_start(which, height):
+        for o in range(1, inner):
+            peer, where = near_peer(o)
+            pltpu.make_async_remote_copy(
+                near_slots.at[which, low_id, pl.ds(0, height)],
+                near_slots.at[which, low_id, pl.ds(0, height)],
+                near_send.at[which, o],
+                near_recv.at[which, low_id],
+                device_id=where,
+                device_id_type=MESH,
+            ).start()
+
+    def near_wait(which, height):
+        for o in range(1, inner):
+            peer, where = near_peer(o)
+            copy = pltpu.make_async_remote_copy(
+                near_slots.at[which, peer, pl.ds(0, height)],
+                near_slots.at[which, peer, pl.ds(0, height)],
+                near_send.at[which, o],
+                near_recv.at[which, peer],
+                device_id=where,
+                device_id_type=MESH,
+            )
+            copy.wait_recv()
+            copy.wait_send()
+
+    def far_start(which, height):
+        for o in range(1, n_far):
+            peer, where = far_peer(o)
+            pltpu.make_async_remote_copy(
+                far_slots.at[which, high_id, pl.ds(0, height)],
+                far_slots.at[which, high_id, pl.ds(0, height)],
+                far_send.at[which, o],
+                far_recv.at[which, high_id],
+                device_id=where,
+                device_id_type=MESH,
+            ).start()
+
+    def far_wait(which, height):
+        for o in range(1, n_far):
+            peer, where = far_peer(o)
+            copy = pltpu.make_async_remote_copy(
+                far_slots.at[which, peer, pl.ds(0, height)],
+                far_slots.at[which, peer, pl.ds(0, height)],
+                far_send.at[which, o],
+                far_recv.at[which, peer],
+                device_id=where,
+                device_id_type=MESH,
+            )
+            copy.wait_recv()
+            copy.wait_send()
+
+    def merge_stats(tiles):
+        lane = iota((8, 128), 1)
+        most, summed = tiles[0], tiles[0]
+        for tile in tiles[1:]:
+            most, summed = jnp.maximum(most, tile), summed + tile
+        return jnp.where(lane == 2, summed, most)
+
+    near_start(0, 8)
+
+    l_forcing.wait()
+
+    def halo_up(k):
+        return pltpu.make_async_remote_copy(
+            basis.at[k, rows], basis.at[k, 0], halo_send.at[k, 0], halo_recv.at[k, 0], device_id=up, device_id_type=MESH
+        )
+
+    def halo_down(k):
+        return pltpu.make_async_remote_copy(
+            basis.at[k, 1], basis.at[k, rows + 1], halo_send.at[k, 1], halo_recv.at[k, 1], device_id=down, device_id_type=MESH
+        )
+
+    def send_halos(k):
+        @pl.when(has_up)
+        def _():
+            halo_up(k).start()
+
+        @pl.when(has_down)
+        def _():
+            halo_down(k).start()
+
+    @pl.when(fluid)
+    def _():
+        pltpu.make_async_remote_copy(
+            picked, walls, contact_send.at[0], contact_recv.at[groups - 1], device_id=(groups - 1, brick), device_id_type=MESH
+        ).wait_recv()
+
+    @pl.when(solid)
+    def _():
+        for g in range(groups - 1):
+            pltpu.make_async_remote_copy(
+                picked, nears.at[g], contact_send.at[g], contact_recv.at[g], device_id=(g, brick), device_id_type=MESH
+            ).wait_recv()
+        walls[...] = nears[0] + nears[1] + nears[2] - picked[...]
+
+    heat = factor[...] * walls[0:lines]
+    extra = spread(jnp.where(solid, heat, heat * owned)).reshape(rows, width, depth)
+    basis[0, 1 : rows + 1] = forcing[...] + extra
+    send_halos(0)
+
+    near_wait(0, 8)
+    far_slots[0, high_id, 0:8] = merge_stats([near_slots[0, i, 0:8] for i in range(inner)])
+    far_start(0, 8)
+
+    def gram_row(k):
+        def body(r, accs):
+            accs = list(accs)
+            for j in range(width // 8):
+                span = slice(8 * j, 8 * j + 8)
+                mine = basis[k, r + 1, span, :]
+                for i in range(k + 1):
+                    other = mine if i == k else basis[i, r + 1, span, :]
+                    accs[i] = accs[i] + mine * other
+            return tuple(accs)
+
+        accs = lax.fori_loop(0, rows, body, tuple(jnp.zeros((8, depth), F32) for _ in range(k + 1)))
+        row, lane = iota((16, 128), 0), iota((16, 128), 1)
+        tile = jnp.zeros((16, 128), F32) if k == 0 else gram_tile[...]
+        for i in range(k + 1):
+            spot = ((row == i) & (lane == k)) | ((row == k) & (lane == i))
+            tile = jnp.where(spot, total(accs[i]), tile)
+        gram_tile[...] = tile
+
+    def local(r, v):
+        return (
+            diag[r] * v
+            - uy[r] * pltpu.roll(v, width - 1, 0)
+            - ly[r] * pltpu.roll(v, 1, 0)
+            - uz[r] * pltpu.roll(v, depth - 1, 1)
+            - lz[r] * pltpu.roll(v, 1, 1)
+        )
+
+    def apply(k, scale):
+        def keep(r, q):
+            if k == 0:
+                basis[1, r + 1] = q
+            else:
+                basis[k + 1, r + 1] = scale * q - basis[k - 1, r + 1]
+
+        @pl.when(fluid)
+        def _():
+            def middle(r, carry):
+                v = basis[k, r + 1]
+                keep(r, local(r, v) - gx[r] * basis[k, r] - ax[r + 1] * basis[k, r + 2])
+                return carry
+
+            keep(0, local(0, basis[k, 1]) - ax[1] * basis[k, 2])
+            keep(rows - 1, local(rows - 1, basis[k, rows]) - gx[rows - 1] * basis[k, rows - 1])
+            lax.fori_loop(1, rows - 1, middle, 0)
+
+        @pl.when(solid)
+        def _():
+            for e in range(width // 8):
+                u = (root[:, 8 * e : 8 * e + 8, :] * basis[k, 1 : rows + 1, 8 * e : 8 * e + 8, :]).reshape(64, depth)
+                high, low = pieces(u)
+                uh[e], ul[e] = high, low
+                stiff[e] = dot(wxy[...], jnp.concatenate([high, low, high], axis=0), ((1,), (0,)))
+            high, low = uh[...].reshape(cells, depth), ul[...].reshape(cells, depth)
+            along = dot(high, wz[0], ((1,), (0,))) + dot(low, wz[0], ((1,), (0,))) + dot(high, wz[1], ((1,), (0,)))
+            stiff[...] = stiff[...] + along.reshape(width // 8, 64, depth)
+
+            def each(r, carry):
+                force = stiff[:, pl.ds(r * 8, 8), :].reshape(width, depth)
+                keep(r, local(r, basis[k, r + 1]) + root[r] * force)
+                return carry
+
+            lax.fori_loop(0, rows, each, 0)
+
+    def finish(k, scale):
+        @pl.when(has_down)
+        def _():
+            halo_up(k).wait_recv()
+
+        @pl.when(has_up)
+        def _():
+            halo_down(k).wait_recv()
+
+        low = gx[0] * basis[k, 0]
+        top = ax[rows] * basis[k, rows + 1]
+        if k == 0:
+            basis[1, 1] = basis[1, 1] - low
+            basis[1, rows] = basis[1, rows] - top
+        else:
+            basis[k + 1, 1] = basis[k + 1, 1] - scale * low
+            basis[k + 1, rows] = basis[k + 1, rows] - scale * top
+
+    apply(0, None)
+    finish(0, None)
+    gram_row(0)
+    far_wait(0, 8)
+    split = (groups - 1) * outer
+
+    def interval(tiles, count):
+        stats = merge_stats(tiles)
+        mean = stats[0:1, 2:3] * (1.0 / count)
+        high = stats[0:1, 0:1] + 0.25 * mean
+        low = jnp.maximum(-stats[0:1, 1:2] - 0.5 * mean, 0.0)
+        return 0.5 * (high + low), 0.5 * (high - low)
+
+    c_fluid, e_fluid = interval([far_slots[0, i, 0:8] for i in range(split)], float((groups - 1) * bricks * cells * depth))
+    c_solid, e_solid = interval([far_slots[0, i, 0:8] for i in range(split, n_far)], float(bricks * cells * depth))
+    center = jnp.where(solid, c_solid, c_fluid)
+    inv_e = 1.0 / jnp.where(solid, e_solid, e_fluid)
+    scale = 2.0 * inv_e
+
+    def rescale(r):
+        basis[1, r + 1] = (basis[1, r + 1] - center * basis[0, r + 1]) * inv_e
+        diag[r] = diag[r] - center
+
+    rescale(0)
+    rescale(rows - 1)
+    send_halos(1)
+
+    def rescale_body(r, carry):
+        rescale(r)
+        return carry
+
+    lax.fori_loop(1, rows - 1, rescale_body, 0)
+    for k in range(1, ITERS):
+        apply(k, scale)
+        gram_row(k)
+        finish(k, scale)
+        if k + 1 < ITERS:
+            send_halos(k + 1)
+    gram_row(ITERS)
+
+    near_slots[1, low_id] = gram_tile[...]
+    near_start(1, 16)
+    near_wait(1, 16)
+    summed = near_slots[1, 0]
+    for i in range(1, inner):
+        summed = summed + near_slots[1, i]
+    far_slots[1, high_id] = summed
+    far_start(1, 16)
+    far_wait(1, 16)
+    gram_fluid = far_slots[1, 0]
+    for i in range(1, split):
+        gram_fluid = gram_fluid + far_slots[1, i]
+    gram_solid = far_slots[1, split]
+    for i in range(split + 1, n_far):
+        gram_solid = gram_solid + far_slots[1, i]
+    y_fluid, ok_fluid = projected(gram_fluid, c_fluid / e_fluid, True)
+    y_solid, ok_solid = projected(gram_solid, c_solid / e_solid, False)
+    coeffs = jnp.where(solid, y_solid, y_fluid) * inv_e
+    flag[...] = jnp.broadcast_to(ok_fluid * ok_solid, (8, 128))
+    weights = [coeffs[k : k + 1, :1] for k in range(ITERS)]
+
+    def combine(r, carry):
+        acc = weights[0] * basis[0, r + 1]
+        for k in range(1, ITERS):
+            acc = acc + weights[k] * basis[k, r + 1]
+        out[r] = acc
+        return carry
+
+    lax.fori_loop(0, rows, combine, 0)
+    stores = [
+        pltpu.make_async_copy(out, out_hbm, store_sem.at[0]),
+        pltpu.make_async_copy(flag, flag_hbm, store_sem.at[1]),
+    ]
+    for store in stores:
+        store.start()
+
+    @pl.when(solid)
+    def _():
+        for g in range(groups - 1):
+            wall_copy(g).wait_send()
+
+    @pl.when(fluid)
+    def _():
+        near_copy.wait_send()
+
+    @pl.when(fluid & has_up)
+    def _():
+        coef_a.wait_send()
+        coef_g.wait_send()
+
+    @pl.when(solid & has_up)
+    def _():
+        coef_up.wait_send()
+
+    @pl.when(solid & has_down)
+    def _():
+        coef_down.wait_send()
+
+    for k in range(ITERS):
+        @pl.when(has_up)
+        def _():
+            halo_up(k).wait_send()
+
+        @pl.when(has_down)
+        def _():
+            halo_down(k).wait_send()
+
+    for store in stores:
+        store.wait()
+
+
+def shards(*arguments):
+    groups, bricks = lax.axis_size("group"), lax.axis_size("brick")
+    forcing = arguments[0]
+    rows, width, depth = slab = forcing.shape
+    lines = arguments[8].shape[0]
+    points = lines * 128
+    n_far = groups * (bricks // 8)
+    vm = pltpu.VMEM
+    scratch = (
+        [vm(slab, F32)] * 3
+        + [vm((3,) + slab, F32)] * 2
+        + [vm(slab, F32)] * 2
+        + [vm((3, 8, 8), F32)]
+        + [vm((lines, 128), jnp.int32)] * 3
+        + [vm((lines, 128), F32)]
+        + [vm((ITERS + 1, rows + 2, width, depth), F32)]
+        + [vm((rows + 1, width, depth), F32)] * 2
+        + [vm(slab, F32)] * 5
+        + [vm((width // 8, 64, depth), F32)]
+        + [vm((width // 8, 64, depth), BF16)] * 2
+        + [vm((2, depth, depth), BF16), vm((64, 192), BF16)]
+        + [vm((width, depth), F32)] * 2
+        + [vm((rows * width, points), BF16), vm((depth, points), BF16)]
+        + [vm((8, 128), F32)] * 2
+        + [vm((groups - 1, 8, 128), F32)]
+        + [vm((16, 128), F32), vm((2, 8, 16, 128), F32), vm((2, n_far, 16, 128), F32)]
+        + [vm(slab, F32), vm((8, 128), F32)]
+    )
+    dma = pltpu.SemaphoreType.DMA
+    semaphores = [
+        dma((12,)),
+        dma((2,)),
+        dma((ITERS, 2)),
+        dma((ITERS, 2)),
+        dma((2,)),
+        dma((2,)),
+        dma((groups,)),
+        dma((groups,)),
+        dma((2, 8)),
+        dma((2, 8)),
+        dma((2, n_far)),
+        dma((2, n_far)),
+    ]
+    result, flag = pl.pallas_call(
+        functools.partial(kernel, groups, bricks),
+        out_shape=(jax.ShapeDtypeStruct(slab, F32), jax.ShapeDtypeStruct((8, 128), F32)),
+        in_specs=[pl.BlockSpec(memory_space=pl.ANY)] * 12,
+        out_specs=(pl.BlockSpec(memory_space=pl.ANY),) * 2,
+        scratch_shapes=scratch + semaphores,
+        compiler_params=pltpu.CompilerParams(collective_id=0, has_side_effects=True, vmem_limit_bytes=56 * 2**20),
+        name="coupled",
+    )(*arguments)
+    return lax.cond(flag[0, 0] > 0.5, lambda: result, lambda: iterated(*arguments))
+
+
 def solution(mesh):
     return jax.shard_map(
         shards,

time: 1650 us -> 70.5 us (0.04)
  blocking collectives: 1350 us -> 0 us
  other arithmetic: 147 us -> 0 us
  Pallas kernels: 0 us -> 66.2 us
  local copies, waits for them, and re-layouts: 58.8 us -> 3.09 us
  between operations: 44.2 us -> 0.75 us
  starting transfers between devices: 26.5 us -> 0 us
    psum x19 -> x0, blocking collectives: 1350 us -> none  [the longest x8 668 us: shards(): lax.psum((inner * fluid_flag, jnp.sum(direction * image) * solid_flag), (...]
    pallas_call x0 -> x1, Pallas kernels: none -> 66.2 us  [shards(): pl.pallas_call(functools.partial(kernel, groups, bricks), out_shape=(jax....]
    reduce_sum x19 -> x0, other arithmetic: 66.1 us -> none  [the longest x6 23.9 us: shards(): jnp.sum(resid * resid) * solid_flag]
    another operation x35 -> x0, local copies, waits for them, and re-layouts: 28 us -> none  [the longest x4 16.8 us: shards(): inner = jnp.stack([jnp.sum(basis[j] * image) for j in range(step + 1)])]
    select_n x11 -> x0, other arithmetic: 26.8 us -> none  [the longest x8 17.1 us: shards(): vector = jnp.where(solid, direction, basis[step])]
    mul x20 -> x0, other arithmetic: 26.6 us -> none  [the longest x8 14.7 us: fluid_branch(): flux_x = face_x * ((1.0 + flow_speed[0]) * vector - following)]
    ppermute x18 -> x0, starting transfers between devices: 26.5 us -> none  [the longest x8 10.9 us: extended(): lax.ppermute(tail, axis, [(i, (i + 1) % count) for i in range(ends)])]
  transfers between devices with their start and end apart: 18 -> 0, of which waited for: 8 -> 0; matrix products, arithmetic and copies ran while one was open for 2% -> 0% of each run, Pallas kernels for 0% -> 0%
where the time goes in v1:
time: 70.5 us; the launch traced here: 70.2 us
  Pallas kernels  66.2 us (94%)
  local copies, waits for them, and re-layouts  3.09 us (4%)
  between operations  0.75 us (1%)
    pallas_call x1, Pallas kernels, shards(): pl.pallas_call(functools.partial(kernel, groups, bricks), out_shape=(jax....  66.2 us
    unnamed x15, local copies, waits for them, and re-layouts  1.9 us

profile of v1, /device:TPU:0, one launch (start us, length us, event | category | flops | bytes accessed | tf_op | source)
XLA Modules:
  0.0 70.2 jit_solution(13485772060555807401)
XLA Ops:
  0.0 0.0 copy-start.82
  0.0 0.0 copy-start.85
  0.0 0.0 copy-start.114
  0.0 0.0 copy-start.131
  0.0 0.0 copy-start.134
  0.0 0.0 copy-start.135
  0.0 0.0 copy-start.136
  0.0 66.2 %coupled.1 = (f32[8,64,256]{2,1,0:T(8,128)}, f32[8,128]{1,0:T(8,128)}) custom-call(f32[8,64,256]{2,1,0:T(8,128)} %forcing_hbm.1, f32[8,64,256]{2,1,0:T(8,128)} %thermal_hbm.1, f32[8,64,256]{2,1,0:T(8,128)} %storage_hbm.1, f32[3,8,64,256]{3,2,1,0:T(8,128)} %opening_hbm.1, f32[3,8,64,256]{3,2,1,0:T(8,128)} %flow_hbm.1, f32[8,64,256]{2,1,0:T(8,128)} %root_hbm.1, ...), custom_call_target="tpu_custom_call" | custom-call | tf_op jit(solution)/shard_map/coupled/pallas_call | solution.py:1001
  66.2 1.2 %slice.1047 = f32[1,1]{1,0:T(1,128)} slice(f32[8,128]{1,0:T(8,128)} %get-tuple-element.751), slice={[0:1], [0:1]} | slice | bytes 8 | tf_op jit(solution)/shard_map/slice | solution.py:1010
  68.0 0.0 copy-done.82
  68.0 0.0 copy-done.85
  68.1 0.0 copy-done.114
  68.1 0.0 copy-done.131
  68.1 0.0 copy-done.134
  68.1 0.0 copy-done.135
  68.1 0.0 copy-done.136
  68.1 0.2 conditional.9
  68.3 1.9 %copy.588 = f32[8,64,256]{2,1,0:T(8,128)} copy(f32[8,64,256]{2,1,0:T(8,128)} %get-tuple-element.753) | data formatting | bytes 1048576
Async XLA Ops:
  0.0 68.0 %copy-start.82 = (f32[3,8,64,256]{3,2,1,0:T(8,128)S(1)}, f32[3,8,64,256]{3,2,1,0:T(8,128)}, u32[]{:S(2)}) copy-start(f32[3,8,64,256]{3,2,1,0:T(8,128)} %opening_hbm.1) | copy-start | bytes 4718596
  0.0 68.0 %copy-start.85 = (f32[8,64,256]{2,1,0:T(8,128)S(1)}, f32[8,64,256]{2,1,0:T(8,128)}, u32[]{:S(2)}) copy-start(f32[8,64,256]{2,1,0:T(8,128)} %weight_hbm.1) | copy-start | bytes 1572868
  0.0 68.1 %copy-start.114 = (f32[3,8,8]{2,1,0:T(8,128)S(1)}, f32[3,8,8]{2,1,0:T(8,128)}, u32[]{:S(2)}) copy-start(f32[3,8,8]{2,1,0:T(8,128)} %rigidity_hbm.1) | copy-start | bytes 2308
  0.0 68.1 %copy-start.131 = (f32[4,128]{1,0:T(4,128)S(1)}, f32[4,128]{1,0:T(4,128)}, u32[]{:S(2)}) copy-start(f32[4,128]{1,0:T(4,128)} %factor_hbm.1) | copy-start | bytes 6148
  0.0 68.1 %copy-start.134 = (s32[4,128]{1,0:T(4,128)S(1)}, s32[4,128]{1,0:T(4,128)}, u32[]{:S(2)}) copy-start(s32[4,128]{1,0:T(4,128)} %volume_hbm.1) | copy-start | bytes 6148
  0.0 68.1 %copy-start.135 = (s32[4,128]{1,0:T(4,128)S(1)}, s32[4,128]{1,0:T(4,128)}, u32[]{:S(2)}) copy-start(s32[4,128]{1,0:T(4,128)} %vertex_hbm.1) | copy-start | bytes 6148
  0.0 68.1 %copy-start.136 = (s32[4,128]{1,0:T(4,128)S(1)}, s32[4,128]{1,0:T(4,128)}, u32[]{:S(2)}) copy-start(s32[4,128]{1,0:T(4,128)} %part_hbm.1) | copy-start | bytes 6148

commit v2 on v1

--- a/solution.py
+++ b/solution.py
@@ -227,6 +227,8 @@
 MESH = pl.DeviceIdType.MESH
 PIVOT_LEAST = 1e-3
 REFINE_MOST = 3e-4
+PARTS = 4
+RAW = {1: ITERS + 1, 2: ITERS + 2}
 
 
 def iota(shape, dim):
@@ -300,6 +302,10 @@
     return coeffs, jnp.where(good, 1.0, 0.0)
 
 
+def ring_far(step, size):
+    return min(step, size - step)
+
+
 def kernel(
     groups,
     bricks,
@@ -316,7 +322,7 @@
     vertex_hbm,
     factor_hbm,
     out_hbm,
-    flag_hbm,
+    flag,
     thermal,
     forcing,
     storage,
@@ -353,7 +359,6 @@
     near_slots,
     far_slots,
     out,
-    flag,
     load_sem,
     store_sem,
     halo_send,
@@ -406,19 +411,23 @@
         load.start()
     (l_vertex, l_volume, l_thermal, l_part, l_factor, l_opening, l_flow, l_storage, l_weight, l_root, l_rigid, l_forcing) = loads
 
-    def near_peer(o):
-        peer = lax.rem(low_id + o, inner)
-        return peer, (group, (brick // inner) * inner + peer)
-
-    def far_peer(o):
-        peer = lax.rem(high_id + o, n_far)
-        return peer, (peer // outer, lax.rem(peer, outer) * inner + low_id)
+    plane_id = brick // inner
+    near_peers, far_peers = [], []
+    for dz, dc in sorted(((a, b) for a in range(inner // 2) for b in range(2)), key=lambda at: -ring_far(at[0], inner // 2)):
+        if dz or dc:
+            peer = lax.rem(low_id // 2 + dz, inner // 2) * 2 + lax.rem(low_id + dc, 2)
+            near_peers.append((peer, (group, plane_id * inner + peer)))
+    steps = sorted(
+        ((a, b) for a in range(groups) for b in range(outer)), key=lambda at: -ring_far(at[0], groups) - ring_far(at[1], outer)
+    )
+    for dx, dy in steps:
+        if dx or dy:
+            x_id, y_id = lax.rem(group + dx, groups), lax.rem(plane_id + dy, outer)
+            far_peers.append((x_id * outer + y_id, (x_id, y_id * inner + low_id)))
 
     barrier = pltpu.get_barrier_semaphore()
-    for o in range(1, inner):
-        pl.semaphore_signal(barrier, inc=1, device_id=near_peer(o)[1], device_id_type=MESH)
-    for o in range(1, n_far):
-        pl.semaphore_signal(barrier, inc=1, device_id=far_peer(o)[1], device_id_type=MESH)
+    for peer, where in far_peers + near_peers:
+        pl.semaphore_signal(barrier, inc=1, device_id=where, device_id_type=MESH)
 
     @pl.when(has_up)
     def _():
@@ -431,12 +440,12 @@
     @pl.when(at_bottom)
     def _():
         for k in range(ITERS):
-            basis[k, 0] = jnp.zeros(plane, F32)
+            basis[RAW.get(k, k), 0] = jnp.zeros(plane, F32)
 
     @pl.when(at_top)
     def _():
         for k in range(ITERS):
-            basis[k, rows + 1] = jnp.zeros(plane, F32)
+            basis[RAW.get(k, k), rows + 1] = jnp.zeros(plane, F32)
 
     l_vertex.wait()
     l_volume.wait()
@@ -658,8 +667,7 @@
         diag[rows - 1] = diag[rows - 1] + ax[rows]
 
     def near_start(which, height):
-        for o in range(1, inner):
-            peer, where = near_peer(o)
+        for o, (peer, where) in enumerate(near_peers):
             pltpu.make_async_remote_copy(
                 near_slots.at[which, low_id, pl.ds(0, height)],
                 near_slots.at[which, low_id, pl.ds(0, height)],
@@ -670,8 +678,7 @@
             ).start()
 
     def near_wait(which, height):
-        for o in range(1, inner):
-            peer, where = near_peer(o)
+        for o, (peer, where) in enumerate(near_peers):
             copy = pltpu.make_async_remote_copy(
                 near_slots.at[which, peer, pl.ds(0, height)],
                 near_slots.at[which, peer, pl.ds(0, height)],
@@ -684,8 +691,7 @@
             copy.wait_send()
 
     def far_start(which, height):
-        for o in range(1, n_far):
-            peer, where = far_peer(o)
+        for o, (peer, where) in enumerate(far_peers):
             pltpu.make_async_remote_copy(
                 far_slots.at[which, high_id, pl.ds(0, height)],
                 far_slots.at[which, high_id, pl.ds(0, height)],
@@ -696,8 +702,7 @@
             ).start()
 
     def far_wait(which, height):
-        for o in range(1, n_far):
-            peer, where = far_peer(o)
+        for o, (peer, where) in enumerate(far_peers):
             copy = pltpu.make_async_remote_copy(
                 far_slots.at[which, peer, pl.ds(0, height)],
                 far_slots.at[which, peer, pl.ds(0, height)],
@@ -720,24 +725,40 @@
 
     l_forcing.wait()
 
-    def halo_up(k):
+    part_rows = width // PARTS
+
+    def halo_up(k, j):
+        span = pl.ds(j * part_rows, part_rows)
+        at = RAW.get(k, k)
         return pltpu.make_async_remote_copy(
-            basis.at[k, rows], basis.at[k, 0], halo_send.at[k, 0], halo_recv.at[k, 0], device_id=up, device_id_type=MESH
+            basis.at[at, rows, span],
+            basis.at[at, 0, span],
+            halo_send.at[k, 0, j],
+            halo_recv.at[k, 0, j],
+            device_id=up,
+            device_id_type=MESH,
         )
 
-    def halo_down(k):
+    def halo_down(k, j):
+        span = pl.ds(j * part_rows, part_rows)
+        at = RAW.get(k, k)
         return pltpu.make_async_remote_copy(
-            basis.at[k, 1], basis.at[k, rows + 1], halo_send.at[k, 1], halo_recv.at[k, 1], device_id=down, device_id_type=MESH
+            basis.at[at, 1, span],
+            basis.at[at, rows + 1, span],
+            halo_send.at[k, 1, j],
+            halo_recv.at[k, 1, j],
+            device_id=down,
+            device_id_type=MESH,
         )
 
-    def send_halos(k):
+    def send_halos(k, j):
         @pl.when(has_up)
         def _():
-            halo_up(k).start()
+            halo_up(k, j).start()
 
         @pl.when(has_down)
         def _():
-            halo_down(k).start()
+            halo_down(k, j).start()
 
     @pl.when(fluid)
     def _():
@@ -756,11 +777,8 @@
     heat = factor[...] * walls[0:lines]
     extra = spread(jnp.where(solid, heat, heat * owned)).reshape(rows, width, depth)
     basis[0, 1 : rows + 1] = forcing[...] + extra
-    send_halos(0)
-
-    near_wait(0, 8)
-    far_slots[0, high_id, 0:8] = merge_stats([near_slots[0, i, 0:8] for i in range(inner)])
-    far_start(0, 8)
+    for j in range(PARTS):
+        send_halos(0, j)
 
     def gram_row(k):
         def body(r, accs):
@@ -791,27 +809,29 @@
         )
 
     def apply(k, scale):
+        at, to = (RAW.get(k, k), RAW[k + 1]) if scale is None else (k, k + 1)
+
         def keep(r, q):
-            if k == 0:
-                basis[1, r + 1] = q
+            if scale is None:
+                basis[to, r + 1] = q
             else:
-                basis[k + 1, r + 1] = scale * q - basis[k - 1, r + 1]
+                basis[to, r + 1] = scale * q - basis[k - 1, r + 1]
 
         @pl.when(fluid)
         def _():
             def middle(r, carry):
-                v = basis[k, r + 1]
-                keep(r, local(r, v) - gx[r] * basis[k, r] - ax[r + 1] * basis[k, r + 2])
+                v = basis[at, r + 1]
+                keep(r, local(r, v) - gx[r] * basis[at, r] - ax[r + 1] * basis[at, r + 2])
                 return carry
 
-            keep(0, local(0, basis[k, 1]) - ax[1] * basis[k, 2])
-            keep(rows - 1, local(rows - 1, basis[k, rows]) - gx[rows - 1] * basis[k, rows - 1])
+            keep(0, local(0, basis[at, 1]) - ax[1] * basis[at, 2])
+            keep(rows - 1, local(rows - 1, basis[at, rows]) - gx[rows - 1] * basis[at, rows - 1])
             lax.fori_loop(1, rows - 1, middle, 0)
 
         @pl.when(solid)
         def _():
             for e in range(width // 8):
-                u = (root[:, 8 * e : 8 * e + 8, :] * basis[k, 1 : rows + 1, 8 * e : 8 * e + 8, :]).reshape(64, depth)
+                u = (root[:, 8 * e : 8 * e + 8, :] * basis[at, 1 : rows + 1, 8 * e : 8 * e + 8, :]).reshape(64, depth)
                 high, low = pieces(u)
                 uh[e], ul[e] = high, low
                 stiff[e] = dot(wxy[...], jnp.concatenate([high, low, high], axis=0), ((1,), (0,)))
@@ -821,32 +841,43 @@
 
             def each(r, carry):
                 force = stiff[:, pl.ds(r * 8, 8), :].reshape(width, depth)
-                keep(r, local(r, basis[k, r + 1]) + root[r] * force)
+                keep(r, local(r, basis[at, r + 1]) + root[r] * force)
                 return carry
 
             lax.fori_loop(0, rows, each, 0)
 
-    def finish(k, scale):
-        @pl.when(has_down)
-        def _():
-            halo_up(k).wait_recv()
-
-        @pl.when(has_up)
-        def _():
-            halo_down(k).wait_recv()
-
-        low = gx[0] * basis[k, 0]
-        top = ax[rows] * basis[k, rows + 1]
-        if k == 0:
-            basis[1, 1] = basis[1, 1] - low
-            basis[1, rows] = basis[1, rows] - top
-        else:
-            basis[k + 1, 1] = basis[k + 1, 1] - scale * low
-            basis[k + 1, rows] = basis[k + 1, rows] - scale * top
+    def finish(k, scale, mix=None):
+        at, to = RAW.get(k, k), (RAW[k + 1] if scale is None else k + 1)
+        for j in range(PARTS):
+            span = slice(j * part_rows, (j + 1) * part_rows)
+
+            @pl.when(has_down)
+            def _():
+                halo_up(k, j).wait_recv()
+
+            @pl.when(has_up)
+            def _():
+                halo_down(k, j).wait_recv()
+
+            for own, halo, coef in ((1, 0, gx.at[0]), (rows, rows + 1, ax.at[rows])):
+                value = basis[at, halo, span]
+                if mix is not None:
+                    value = mix[0] * value + mix[1] * basis[RAW[1], halo, span] + mix[2] * basis[0, halo, span]
+                value = coef[span] * value
+                if scale is not None:
+                    value = scale * value
+                basis[to, own, span] = basis[to, own, span] - value
+            if k + 1 < ITERS:
+                send_halos(k + 1, j)
 
     apply(0, None)
+    near_wait(0, 8)
+    far_slots[0, high_id, 0:8] = merge_stats([near_slots[0, i, 0:8] for i in range(inner)])
+    far_start(0, 8)
     finish(0, None)
+    apply(1, None)
     gram_row(0)
+    finish(1, None)
     far_wait(0, 8)
     split = (groups - 1) * outer
 
@@ -863,25 +894,22 @@
     inv_e = 1.0 / jnp.where(solid, e_solid, e_fluid)
     scale = 2.0 * inv_e
 
-    def rescale(r):
-        basis[1, r + 1] = (basis[1, r + 1] - center * basis[0, r + 1]) * inv_e
+    mix = (scale * inv_e, -2.0 * scale * center * inv_e, scale * inv_e * center * center - 1.0)
+
+    def convert(r, carry):
+        zero, one, two = basis[0, r + 1], basis[RAW[1], r + 1], basis[RAW[2], r + 1]
+        basis[1, r + 1] = (one - center * zero) * inv_e
+        basis[2, r + 1] = mix[0] * two + mix[1] * one + mix[2] * zero
         diag[r] = diag[r] - center
-
-    rescale(0)
-    rescale(rows - 1)
-    send_halos(1)
-
-    def rescale_body(r, carry):
-        rescale(r)
         return carry
 
-    lax.fori_loop(1, rows - 1, rescale_body, 0)
-    for k in range(1, ITERS):
+    lax.fori_loop(0, rows, convert, 0)
+    for k in range(2, ITERS):
         apply(k, scale)
+        if k == 2:
+            gram_row(1)
         gram_row(k)
-        finish(k, scale)
-        if k + 1 < ITERS:
-            send_halos(k + 1)
+        finish(k, scale, mix if k == 2 else None)
     gram_row(ITERS)
 
     near_slots[1, low_id] = gram_tile[...]
@@ -902,7 +930,7 @@
     y_fluid, ok_fluid = projected(gram_fluid, c_fluid / e_fluid, True)
     y_solid, ok_solid = projected(gram_solid, c_solid / e_solid, False)
     coeffs = jnp.where(solid, y_solid, y_fluid) * inv_e
-    flag[...] = jnp.broadcast_to(ok_fluid * ok_solid, (8, 128))
+    flag[0] = jnp.max(ok_fluid * ok_solid).astype(jnp.int32)
     weights = [coeffs[k : k + 1, :1] for k in range(ITERS)]
 
     def combine(r, carry):
@@ -913,12 +941,8 @@
         return carry
 
     lax.fori_loop(0, rows, combine, 0)
-    stores = [
-        pltpu.make_async_copy(out, out_hbm, store_sem.at[0]),
-        pltpu.make_async_copy(flag, flag_hbm, store_sem.at[1]),
-    ]
-    for store in stores:
-        store.start()
+    store = pltpu.make_async_copy(out, out_hbm, store_sem)
+    store.start()
 
     @pl.when(solid)
     def _():
@@ -943,16 +967,33 @@
         coef_down.wait_send()
 
     for k in range(ITERS):
-        @pl.when(has_up)
-        def _():
-            halo_up(k).wait_send()
-
-        @pl.when(has_down)
-        def _():
-            halo_down(k).wait_send()
-
-    for store in stores:
-        store.wait()
+        for j in range(PARTS):
+
+            @pl.when(has_up)
+            def _():
+                halo_up(k, j).wait_send()
+
+            @pl.when(has_down)
+            def _():
+                halo_down(k, j).wait_send()
+
+    store.wait()
+
+
+def handed_on(result):
+    def body(source, target, sem):
+        copy = pltpu.make_async_copy(source, target, sem)
+        copy.start()
+        copy.wait()
+
+    return pl.pallas_call(
+        body,
+        out_shape=jax.ShapeDtypeStruct(result.shape, result.dtype),
+        in_specs=[pl.BlockSpec(memory_space=pl.ANY)],
+        out_specs=pl.BlockSpec(memory_space=pl.ANY),
+        scratch_shapes=[pltpu.SemaphoreType.DMA],
+        name="handed_on",
+    )(result)
 
 
 def shards(*arguments):
@@ -970,7 +1011,7 @@
         + [vm((3, 8, 8), F32)]
         + [vm((lines, 128), jnp.int32)] * 3
         + [vm((lines, 128), F32)]
-        + [vm((ITERS + 1, rows + 2, width, depth), F32)]
+        + [vm((ITERS + 3, rows + 2, width, depth), F32)]
         + [vm((rows + 1, width, depth), F32)] * 2
         + [vm(slab, F32)] * 5
         + [vm((width // 8, 64, depth), F32)]
@@ -981,14 +1022,14 @@
         + [vm((8, 128), F32)] * 2
         + [vm((groups - 1, 8, 128), F32)]
         + [vm((16, 128), F32), vm((2, 8, 16, 128), F32), vm((2, n_far, 16, 128), F32)]
-        + [vm(slab, F32), vm((8, 128), F32)]
+        + [vm(slab, F32)]
     )
     dma = pltpu.SemaphoreType.DMA
     semaphores = [
         dma((12,)),
-        dma((2,)),
-        dma((ITERS, 2)),
-        dma((ITERS, 2)),
+        dma,
+        dma((ITERS, 2, PARTS)),
+        dma((ITERS, 2, PARTS)),
         dma((2,)),
         dma((2,)),
         dma((groups,)),
@@ -1000,14 +1041,14 @@
     ]
     result, flag = pl.pallas_call(
         functools.partial(kernel, groups, bricks),
-        out_shape=(jax.ShapeDtypeStruct(slab, F32), jax.ShapeDtypeStruct((8, 128), F32)),
+        out_shape=(jax.ShapeDtypeStruct(slab, F32), jax.ShapeDtypeStruct((1,), jnp.int32)),
         in_specs=[pl.BlockSpec(memory_space=pl.ANY)] * 12,
-        out_specs=(pl.BlockSpec(memory_space=pl.ANY),) * 2,
+        out_specs=(pl.BlockSpec(memory_space=pl.ANY), pl.BlockSpec(memory_space=pltpu.SMEM)),
         scratch_shapes=scratch + semaphores,
         compiler_params=pltpu.CompilerParams(collective_id=0, has_side_effects=True, vmem_limit_bytes=56 * 2**20),
         name="coupled",
     )(*arguments)
-    return lax.cond(flag[0, 0] > 0.5, lambda: result, lambda: iterated(*arguments))
+    return lax.cond(flag[0] > 0, lambda: handed_on(result), lambda: iterated(*arguments))
 
 
 def solution(mesh):

time: 70.5 us -> 81.1 us (1.15)
  Pallas kernels: 66.2 us -> 79.4 us
  local copies, waits for them, and re-layouts: 3.09 us -> 0.03 us
    pallas_call x0 -> x1, Pallas kernels: none -> 17 us  [handed_on(): pl.pallas_call(body, out_shape=jax.ShapeDtypeStruct(result.shape, result....]
    pallas_call x1, Pallas kernels: 66.2 us -> 62.4 us  [shards(): pl.pallas_call(functools.partial(kernel, groups, bricks), out_shape=(jax....]
    unnamed x15 -> x14, local copies, waits for them, and re-layouts: 1.9 us -> 0.03 us
    slice x1 -> x0, local copies, waits for them, and re-layouts: 1.19 us -> none  [shards(): flag[0, 0] > 0.5]
where the time goes in v2:
time: 81.1 us; the launch traced here: 80.7 us
  Pallas kernels  79.4 us (98%)
  between operations  0.99 us (1%)
    pallas_call x1, Pallas kernels, shards(): pl.pallas_call(functools.partial(kernel, groups, bricks), out_shape=(jax....  62.4 us
    pallas_call x1, Pallas kernels, handed_on(): pl.pallas_call(body, out_shape=jax.ShapeDtypeStruct(result.shape, result....  17 us

profile of v2, /device:TPU:0, one launch (start us, length us, event | category | flops | bytes accessed | tf_op | source)
XLA Modules:
  0.0 80.7 jit_solution(9084580274222646516)
XLA Ops:
  0.0 0.0 copy-start.82
  0.0 0.0 copy-start.85
  0.0 0.0 copy-start.114
  0.0 0.0 copy-start.131
  0.0 0.0 copy-start.134
  0.0 0.0 copy-start.135
  0.0 0.0 copy-start.136
  0.0 62.4 %coupled.1 = (f32[8,64,256]{2,1,0:T(8,128)}, s32[1]{0:T(128)}) custom-call(f32[8,64,256]{2,1,0:T(8,128)} %forcing_hbm.1, f32[8,64,256]{2,1,0:T(8,128)} %thermal_hbm.1, f32[8,64,256]{2,1,0:T(8,128)} %storage_hbm.1, f32[3,8,64,256]{3,2,1,0:T(8,128)} %opening_hbm.1, f32[3,8,64,256]{3,2,1,0:T(8,128)} %flow_hbm.1, f32[8,64,256]{2,1,0:T(8,128)} %root_hbm.1, ...), custom_call_target="tpu_custom_call" | custom-call | tf_op jit(solution)/shard_map/coupled/pallas_call | solution.py:1042
  63.2 0.0 copy-done.82
  63.2 0.0 copy-done.85
  63.2 0.0 copy-done.114
  63.2 0.0 copy-done.131
  63.2 0.0 copy-done.134
  63.2 0.0 copy-done.135
  63.2 0.0 copy-done.136
  63.2 17.2 %conditional.9 = (f32[8,64,256]{2,1,0:T(8,128)}) conditional(s32[]{:T(128)} %bitcast.271, (f32[8,64,256]{2,1,0:T(8,128)}, s32[4,128]{1,0:T(4,128)S(1)}, s32[4,128]{1,0:T(4,128)S(1)}, s32[4,128]{1,0:T(4,128)S(1)}, f32[8,64,256]{2,1,0:T(8,128)}, /*index=5*/f32[4,128]{1,0:T(4,128)S(1)}, f32[3,8,64,256]{3,2,1,0:T(8,128)S(1)}, ...), branch_computations={%region_0.116_spmd, %region_116.117_spmd} | conditional | flops 1876583936 | bytes 522460992 | solution.py:1051
  63.5 17.0 %handed_on.1 = f32[8,64,256]{2,1,0:T(8,128)} custom-call(f32[8,64,256]{2,1,0:T(8,128)} %source), custom_call_target="tpu_custom_call" | custom-call | tf_op jit(solution)/shard_map/cond/branch_1_fun/handed_on/pallas_call | solution.py:989
Async XLA Ops:
  0.0 63.2 %copy-start.82 = (f32[3,8,64,256]{3,2,1,0:T(8,128)S(1)}, f32[3,8,64,256]{3,2,1,0:T(8,128)}, u32[]{:S(2)}) copy-start(f32[3,8,64,256]{3,2,1,0:T(8,128)} %opening_hbm.1) | copy-start | bytes 4718596
  0.0 63.2 %copy-start.85 = (f32[8,64,256]{2,1,0:T(8,128)S(1)}, f32[8,64,256]{2,1,0:T(8,128)}, u32[]{:S(2)}) copy-start(f32[8,64,256]{2,1,0:T(8,128)} %weight_hbm.1) | copy-start | bytes 1572868
  0.0 63.2 %copy-start.114 = (f32[3,8,8]{2,1,0:T(8,128)S(1)}, f32[3,8,8]{2,1,0:T(8,128)}, u32[]{:S(2)}) copy-start(f32[3,8,8]{2,1,0:T(8,128)} %rigidity_hbm.1) | copy-start | bytes 2308
  0.0 63.2 %copy-start.131 = (f32[4,128]{1,0:T(4,128)S(1)}, f32[4,128]{1,0:T(4,128)}, u32[]{:S(2)}) copy-start(f32[4,128]{1,0:T(4,128)} %factor_hbm.1) | copy-start | bytes 6148
  0.0 63.2 %copy-start.134 = (s32[4,128]{1,0:T(4,128)S(1)}, s32[4,128]{1,0:T(4,128)}, u32[]{:S(2)}) copy-start(s32[4,128]{1,0:T(4,128)} %volume_hbm.1) | copy-start | bytes 6148
  0.0 63.2 %copy-start.135 = (s32[4,128]{1,0:T(4,128)S(1)}, s32[4,128]{1,0:T(4,128)}, u32[]{:S(2)}) copy-start(s32[4,128]{1,0:T(4,128)} %vertex_hbm.1) | copy-start | bytes 6148
  0.0 63.2 %copy-start.136 = (s32[4,128]{1,0:T(4,128)S(1)}, s32[4,128]{1,0:T(4,128)}, u32[]{:S(2)}) copy-start(s32[4,128]{1,0:T(4,128)} %part_hbm.1) | copy-start | bytes 6148

commit v3 on v2

--- a/solution.py
+++ b/solution.py
@@ -554,24 +554,6 @@
         extra = spread(factor[...] * owned).reshape(rows, width, depth)
         storage[...] = storage[...] + extra
 
-        def first(r, carry):
-            a = opening[0, r]
-            ax[r + 1] = a
-            gx[r + 1] = a * (1.0 + flow[0, r])
-            return carry
-
-        lax.fori_loop(0, rows - 1, first, 0)
-
-        @pl.when(has_down)
-        def _():
-            coef_a.wait_recv()
-            coef_g.wait_recv()
-
-        @pl.when(at_bottom)
-        def _():
-            ax[0] = jnp.zeros(plane, F32)
-            gx[0] = jnp.zeros(plane, F32)
-
         def second(r, carry):
             d_max, d_min, o_sum = carry
             a_y = jnp.where(y_at == width - 1, 0.0, opening[1, r])
@@ -579,8 +561,16 @@
             g_low = pltpu.roll(g_y, 1, 0)
             uy[r] = a_y
             ly[r] = g_low
-            d = storage[r] + ax[r] + gx[r + 1] + g_y + pltpu.roll(a_y, 1, 0)
-            o = ax[r + 1] + gx[r] + a_y + g_low
+            a_x = jnp.where(at_top & (r == rows - 1), 0.0, opening[0, r])
+            g_x = a_x * (1.0 + flow[0, r])
+
+            @pl.when(r < rows - 1)
+            def _():
+                ax[r + 1] = a_x
+                gx[r + 1] = g_x
+
+            d = storage[r] + g_x + g_y + pltpu.roll(a_y, 1, 0)
+            o = a_x + g_x + a_y + g_low
             a_z = jnp.where(z_at == depth - 1, 0.0, opening[2, r])
             g_z = a_z * (1.0 + flow[2, r])
             g_low = pltpu.roll(g_z, 1, 1)
@@ -588,6 +578,7 @@
             lz[r] = g_low
             d = d + g_z + pltpu.roll(a_z, 1, 1)
             o = o + a_z + g_low
+            d = d + jnp.where(r == 0, 0.0, opening[0, jnp.maximum(r - 1, 0)])
             diag[r] = d
             return jnp.maximum(d_max, fold(d, jnp.max)), jnp.minimum(d_min, fold(d, jnp.min)), o_sum + fold(o, jnp.sum)
 
@@ -623,24 +614,6 @@
         mixed = jnp.where(same_y, expand(rigidity[0], outer_x), 0.0) + jnp.where(same_x, expand(rigidity[1], inner_y), 0.0)
         high, low = pieces(mixed)
         wxy[...] = jnp.concatenate([high, high, low], axis=1)
-
-        @pl.when(has_down)
-        def _():
-            coef_up.wait_recv()
-            gx[0] = 0.5 * (weight_low[...] + weight[0])
-
-        @pl.when(at_bottom)
-        def _():
-            gx[0] = jnp.zeros(plane, F32)
-
-        @pl.when(has_up)
-        def _():
-            coef_down.wait_recv()
-            ax[rows] = 0.5 * (weight[rows - 1] + weight_up[...])
-
-        @pl.when(at_top)
-        def _():
-            ax[rows] = jnp.zeros(plane, F32)
 
         def second(r, carry):
             d_max, d_min, o_sum = carry
@@ -663,8 +636,6 @@
             return jnp.maximum(d_max, fold(whole, jnp.max)), jnp.minimum(d_min, fold(whole, jnp.min)), o_sum + fold(o, jnp.sum)
 
         write_stats(*lax.fori_loop(0, rows, second, start))
-        diag[0] = diag[0] + gx[0]
-        diag[rows - 1] = diag[rows - 1] + ax[rows]
 
     def near_start(which, height):
         for o, (peer, where) in enumerate(near_peers):
@@ -779,6 +750,32 @@
     basis[0, 1 : rows + 1] = forcing[...] + extra
     for j in range(PARTS):
         send_halos(0, j)
+
+    @pl.when(at_bottom)
+    def _():
+        gx[0] = jnp.zeros(plane, F32)
+
+    @pl.when(fluid & has_down)
+    def _():
+        coef_a.wait_recv()
+        coef_g.wait_recv()
+        diag[0] = diag[0] + ax[0]
+
+    @pl.when(solid & has_down)
+    def _():
+        coef_up.wait_recv()
+        gx[0] = 0.5 * (weight_low[...] + weight[0])
+        diag[0] = diag[0] + gx[0]
+
+    @pl.when(solid & has_up)
+    def _():
+        coef_down.wait_recv()
+        ax[rows] = 0.5 * (weight[rows - 1] + weight_up[...])
+        diag[rows - 1] = diag[rows - 1] + ax[rows]
+
+    @pl.when(solid & at_top)
+    def _():
+        ax[rows] = jnp.zeros(plane, F32)
 
     def gram_row(k):
         def body(r, accs):
@@ -938,11 +935,10 @@
         for k in range(1, ITERS):
             acc = acc + weights[k] * basis[k, r + 1]
         out[r] = acc
+        pltpu.make_async_copy(out.at[r], out_hbm.at[r], store_sem.at[r]).start()
         return carry
 
     lax.fori_loop(0, rows, combine, 0)
-    store = pltpu.make_async_copy(out, out_hbm, store_sem)
-    store.start()
 
     @pl.when(solid)
     def _():
@@ -977,21 +973,30 @@
             def _():
                 halo_down(k, j).wait_send()
 
-    store.wait()
+    for r in range(rows):
+        pltpu.make_async_copy(out.at[r], out_hbm.at[r], store_sem.at[r]).wait()
 
 
 def handed_on(result):
-    def body(source, target, sem):
-        copy = pltpu.make_async_copy(source, target, sem)
-        copy.start()
-        copy.wait()
+    rows = result.shape[0]
+
+    def body(source, target, held, in_sem, out_sem):
+        ins = [pltpu.make_async_copy(source.at[i], held.at[i], in_sem.at[i]) for i in range(rows)]
+        outs = [pltpu.make_async_copy(held.at[i], target.at[i], out_sem.at[i]) for i in range(rows)]
+        for copy in ins:
+            copy.start()
+        for arrived, copy in zip(ins, outs):
+            arrived.wait()
+            copy.start()
+        for copy in outs:
+            copy.wait()
 
     return pl.pallas_call(
         body,
         out_shape=jax.ShapeDtypeStruct(result.shape, result.dtype),
         in_specs=[pl.BlockSpec(memory_space=pl.ANY)],
         out_specs=pl.BlockSpec(memory_space=pl.ANY),
-        scratch_shapes=[pltpu.SemaphoreType.DMA],
+        scratch_shapes=[pltpu.VMEM(result.shape, F32), pltpu.SemaphoreType.DMA((rows,)), pltpu.SemaphoreType.DMA((rows,))],
         name="handed_on",
     )(result)
 
@@ -1027,7 +1032,7 @@
     dma = pltpu.SemaphoreType.DMA
     semaphores = [
         dma((12,)),
-        dma,
+        dma((rows,)),
         dma((ITERS, 2, PARTS)),
         dma((ITERS, 2, PARTS)),
         dma((2,)),

time: 81.1 us -> 62.2 us (0.77)
  Pallas kernels: 79.4 us -> 60.8 us
    pallas_call x1, Pallas kernels: 17 us -> 1.83 us  [handed_on(): pl.pallas_call(body, out_shape=jax.ShapeDtypeStruct(result.shape, result....]
    pallas_call x1, Pallas kernels: 62.4 us -> 58.9 us  [shards(): pl.pallas_call(functools.partial(kernel, groups, bricks), out_shape=(jax....]
where the time goes in v3:
time: 62.2 us; the launch traced here: 62 us
  Pallas kernels  60.8 us (98%)
  between operations  0.99 us (2%)
    pallas_call x1, Pallas kernels, shards(): pl.pallas_call(functools.partial(kernel, groups, bricks), out_shape=(jax....  58.9 us
    pallas_call x1, Pallas kernels, handed_on(): pl.pallas_call(body, out_shape=jax.ShapeDtypeStruct(result.shape, result....  1.83 us

profile of v3, /device:TPU:0, one launch (start us, length us, event | category | flops | bytes accessed | tf_op | source)
XLA Modules:
  0.0 62.0 jit_solution(1781141357436910937)
XLA Ops:
  0.0 0.0 copy-start.82
  0.0 0.0 copy-start.85
  0.0 0.0 copy-start.114
  0.0 0.0 copy-start.131
  0.0 0.0 copy-start.134
  0.0 0.0 copy-start.135
  0.0 0.0 copy-start.136
  0.0 58.9 %coupled.1 = (f32[8,64,256]{2,1,0:T(8,128)}, s32[1]{0:T(128)}) custom-call(f32[8,64,256]{2,1,0:T(8,128)} %forcing_hbm.1, f32[8,64,256]{2,1,0:T(8,128)} %thermal_hbm.1, f32[8,64,256]{2,1,0:T(8,128)} %storage_hbm.1, f32[3,8,64,256]{3,2,1,0:T(8,128)} %opening_hbm.1, f32[3,8,64,256]{3,2,1,0:T(8,128)} %flow_hbm.1, f32[8,64,256]{2,1,0:T(8,128)} %root_hbm.1, ...), custom_call_target="tpu_custom_call" | custom-call | tf_op jit(solution)/shard_map/coupled/pallas_call | solution.py:1047
  59.7 0.0 copy-done.82
  59.7 0.0 copy-done.85
  59.7 0.0 copy-done.114
  59.7 0.0 copy-done.131
  59.7 0.0 copy-done.134
  59.7 0.0 copy-done.135
  59.7 0.0 copy-done.136
  59.7 2.0 %conditional.9 = (f32[8,64,256]{2,1,0:T(8,128)}) conditional(s32[]{:T(128)} %bitcast.271, (f32[8,64,256]{2,1,0:T(8,128)}, s32[4,128]{1,0:T(4,128)S(1)}, s32[4,128]{1,0:T(4,128)S(1)}, s32[4,128]{1,0:T(4,128)S(1)}, f32[8,64,256]{2,1,0:T(8,128)}, /*index=5*/f32[4,128]{1,0:T(4,128)S(1)}, f32[3,8,64,256]{3,2,1,0:T(8,128)S(1)}, ...), branch_computations={%region_0.116_spmd, %region_116.117_spmd} | conditional | flops 1876583936 | bytes 522460992 | solution.py:1056
  59.9 1.8 %handed_on.1 = f32[8,64,256]{2,1,0:T(8,128)} custom-call(f32[8,64,256]{2,1,0:T(8,128)} %source), custom_call_target="tpu_custom_call" | custom-call | tf_op jit(solution)/shard_map/cond/branch_1_fun/handed_on/pallas_call | solution.py:994
Async XLA Ops:
  0.0 59.7 %copy-start.82 = (f32[3,8,64,256]{3,2,1,0:T(8,128)S(1)}, f32[3,8,64,256]{3,2,1,0:T(8,128)}, u32[]{:S(2)}) copy-start(f32[3,8,64,256]{3,2,1,0:T(8,128)} %opening_hbm.1) | copy-start | bytes 4718596
  0.0 59.7 %copy-start.85 = (f32[8,64,256]{2,1,0:T(8,128)S(1)}, f32[8,64,256]{2,1,0:T(8,128)}, u32[]{:S(2)}) copy-start(f32[8,64,256]{2,1,0:T(8,128)} %weight_hbm.1) | copy-start | bytes 1572868
  0.0 59.7 %copy-start.114 = (f32[3,8,8]{2,1,0:T(8,128)S(1)}, f32[3,8,8]{2,1,0:T(8,128)}, u32[]{:S(2)}) copy-start(f32[3,8,8]{2,1,0:T(8,128)} %rigidity_hbm.1) | copy-start | bytes 2308
  0.0 59.7 %copy-start.131 = (f32[4,128]{1,0:T(4,128)S(1)}, f32[4,128]{1,0:T(4,128)}, u32[]{:S(2)}) copy-start(f32[4,128]{1,0:T(4,128)} %factor_hbm.1) | copy-start | bytes 6148
  0.0 59.7 %copy-start.134 = (s32[4,128]{1,0:T(4,128)S(1)}, s32[4,128]{1,0:T(4,128)}, u32[]{:S(2)}) copy-start(s32[4,128]{1,0:T(4,128)} %volume_hbm.1) | copy-start | bytes 6148
  0.0 59.7 %copy-start.135 = (s32[4,128]{1,0:T(4,128)S(1)}, s32[4,128]{1,0:T(4,128)}, u32[]{:S(2)}) copy-start(s32[4,128]{1,0:T(4,128)} %vertex_hbm.1) | copy-start | bytes 6148
  0.0 59.7 %copy-start.136 = (s32[4,128]{1,0:T(4,128)S(1)}, s32[4,128]{1,0:T(4,128)}, u32[]{:S(2)}) copy-start(s32[4,128]{1,0:T(4,128)} %part_hbm.1) | copy-start | bytes 6148

commit v4 on v3

--- a/solution.py
+++ b/solution.py
@@ -229,6 +229,8 @@
 REFINE_MOST = 3e-4
 PARTS = 4
 RAW = {1: ITERS + 1, 2: ITERS + 2}
+DEEP = (3, 5)
+SKIP = tuple(k + 1 for k in DEEP)
 
 
 def iota(shape, dim):
@@ -359,6 +361,9 @@
     near_slots,
     far_slots,
     out,
+    second,
+    ghost,
+    ghost_diag,
     load_sem,
     store_sem,
     halo_send,
@@ -371,6 +376,10 @@
     near_recv,
     far_send,
     far_recv,
+    deep_send,
+    deep_recv,
+    ghost_send,
+    ghost_recv,
 ):
     group = lax.axis_index("group")
     brick = lax.axis_index("brick")
@@ -386,6 +395,8 @@
     at_top = (brick == bricks - 1) & (group >= groups - 2)
     at_bottom = (brick == 0) & ((group == 0) | (group == groups - 1))
     has_up, has_down = jnp.logical_not(at_top), jnp.logical_not(at_bottom)
+    far_up = (brick == bricks - 1) & (group < groups - 2)
+    far_down = (brick == 0) & (group > 0) & fluid
     device = group * bricks + brick
     up_id = lax.rem(device + 1, groups * bricks)
     down_id = lax.rem(device + groups * bricks - 1, groups * bricks)
@@ -722,14 +733,52 @@
             device_id_type=MESH,
         )
 
+    def linked(k):
+        if k in SKIP:
+            return has_up & jnp.logical_not(far_up), has_down & jnp.logical_not(far_down)
+        return has_up, has_down
+
     def send_halos(k, j):
-        @pl.when(has_up)
+        to_up, to_down = linked(k)
+
+        @pl.when(to_up)
         def _():
             halo_up(k, j).start()
 
-        @pl.when(has_down)
+        @pl.when(to_down)
         def _():
             halo_down(k, j).start()
+
+    def deep_up(i):
+        return pltpu.make_async_remote_copy(
+            basis.at[DEEP[i], rows - 1], second.at[0, i], deep_send.at[i, 0], deep_recv.at[i, 0], device_id=up, device_id_type=MESH
+        )
+
+    def deep_down(i):
+        return pltpu.make_async_remote_copy(
+            basis.at[DEEP[i], 2], second.at[1, i], deep_send.at[i, 1], deep_recv.at[i, 1], device_id=down, device_id_type=MESH
+        )
+
+    def ghost_up(i):
+        source = (ghost_diag.at[0], uy.at[rows - 1], ly.at[rows - 1], uz.at[rows - 1], lz.at[rows - 1], gx.at[rows - 1])[i]
+        return pltpu.make_async_remote_copy(
+            source, ghost.at[0, i], ghost_send.at[0, i], ghost_recv.at[0, i], device_id=up, device_id_type=MESH
+        )
+
+    def ghost_down(i):
+        source = (ghost_diag.at[1], uy.at[0], ly.at[0], uz.at[0], lz.at[0], ax.at[1])[i]
+        return pltpu.make_async_remote_copy(
+            source, ghost.at[1, i], ghost_send.at[1, i], ghost_recv.at[1, i], device_id=down, device_id_type=MESH
+        )
+
+    def send_deep(i):
+        @pl.when(far_up)
+        def _():
+            deep_up(i).start()
+
+        @pl.when(far_down)
+        def _():
+            deep_down(i).start()
 
     @pl.when(fluid)
     def _():
@@ -848,11 +897,13 @@
         for j in range(PARTS):
             span = slice(j * part_rows, (j + 1) * part_rows)
 
-            @pl.when(has_down)
+            from_up, from_down = linked(k)
+
+            @pl.when(from_down)
             def _():
                 halo_up(k, j).wait_recv()
 
-            @pl.when(has_up)
+            @pl.when(from_up)
             def _():
                 halo_down(k, j).wait_recv()
 
@@ -860,6 +911,7 @@
                 value = basis[at, halo, span]
                 if mix is not None:
                     value = mix[0] * value + mix[1] * basis[RAW[1], halo, span] + mix[2] * basis[0, halo, span]
+                    basis[k, halo, span] = value
                 value = coef[span] * value
                 if scale is not None:
                     value = scale * value
@@ -867,11 +919,56 @@
             if k + 1 < ITERS:
                 send_halos(k + 1, j)
 
+    def extend(i):
+        k = DEEP[i]
+
+        def row(side, near, halo, inward):
+            v = basis[k, halo]
+            q = (
+                (ghost[side, 0] - center) * v
+                - ghost[side, 1] * pltpu.roll(v, width - 1, 0)
+                - ghost[side, 2] * pltpu.roll(v, 1, 0)
+                - ghost[side, 3] * pltpu.roll(v, depth - 1, 1)
+                - ghost[side, 4] * pltpu.roll(v, 1, 1)
+                - ghost[side, 5] * second[side, i]
+                - inward * basis[k, near]
+            )
+            basis[k + 1, halo] = scale * q - basis[k - 1, halo]
+
+        @pl.when(far_down)
+        def _():
+            deep_up(i).wait_recv()
+            if i == 0:
+                for n in range(6):
+                    ghost_up(n).wait_recv()
+            row(0, 1, 0, ax[0])
+
+        @pl.when(far_up)
+        def _():
+            deep_down(i).wait_recv()
+            if i == 0:
+                for n in range(6):
+                    ghost_down(n).wait_recv()
+            row(1, rows, rows + 1, gx[rows])
+
     apply(0, None)
     near_wait(0, 8)
     far_slots[0, high_id, 0:8] = merge_stats([near_slots[0, i, 0:8] for i in range(inner)])
     far_start(0, 8)
     finish(0, None)
+
+    @pl.when(far_up)
+    def _():
+        ghost_diag[0] = diag[rows - 1]
+        for n in range(6):
+            ghost_up(n).start()
+
+    @pl.when(far_down)
+    def _():
+        ghost_diag[1] = diag[0]
+        for n in range(6):
+            ghost_down(n).start()
+
     apply(1, None)
     gram_row(0)
     finish(1, None)
@@ -903,10 +1000,14 @@
     lax.fori_loop(0, rows, convert, 0)
     for k in range(2, ITERS):
         apply(k, scale)
+        if k + 1 in DEEP:
+            send_deep(DEEP.index(k + 1))
         if k == 2:
             gram_row(1)
         gram_row(k)
         finish(k, scale, mix if k == 2 else None)
+        if k in DEEP:
+            extend(DEEP.index(k))
     gram_row(ITERS)
 
     near_slots[1, low_id] = gram_tile[...]
@@ -962,14 +1063,29 @@
     def _():
         coef_down.wait_send()
 
+    @pl.when(far_up)
+    def _():
+        for n in range(6):
+            ghost_up(n).wait_send()
+        for i in range(len(DEEP)):
+            deep_up(i).wait_send()
+
+    @pl.when(far_down)
+    def _():
+        for n in range(6):
+            ghost_down(n).wait_send()
+        for i in range(len(DEEP)):
+            deep_down(i).wait_send()
+
     for k in range(ITERS):
+        sent_up, sent_down = linked(k)
         for j in range(PARTS):
 
-            @pl.when(has_up)
+            @pl.when(sent_up)
             def _():
                 halo_up(k, j).wait_send()
 
-            @pl.when(has_down)
+            @pl.when(sent_down)
             def _():
                 halo_down(k, j).wait_send()
 
@@ -1028,6 +1144,7 @@
         + [vm((groups - 1, 8, 128), F32)]
         + [vm((16, 128), F32), vm((2, 8, 16, 128), F32), vm((2, n_far, 16, 128), F32)]
         + [vm(slab, F32)]
+        + [vm((2, len(DEEP), width, depth), F32), vm((2, 6, width, depth), F32), vm((2, width, depth), F32)]
     )
     dma = pltpu.SemaphoreType.DMA
     semaphores = [
@@ -1043,6 +1160,10 @@
         dma((2, 8)),
         dma((2, n_far)),
         dma((2, n_far)),
+        dma((len(DEEP), 2)),
+        dma((len(DEEP), 2)),
+        dma((2, 6)),
+        dma((2, 6)),
     ]
     result, flag = pl.pallas_call(
         functools.partial(kernel, groups, bricks),

time: 62.2 us -> 58.1 us (0.934)
  Pallas kernels: 60.8 us -> 56.6 us
    pallas_call x1, Pallas kernels: 58.9 us -> 54.8 us  [shards(): pl.pallas_call(functools.partial(kernel, groups, bricks), out_shape=(jax....]
where the time goes in v4:
time: 58.1 us; the launch traced here: 57.9 us
  Pallas kernels  56.6 us (97%)
  between operations  0.99 us (2%)
    pallas_call x1, Pallas kernels, shards(): pl.pallas_call(functools.partial(kernel, groups, bricks), out_shape=(jax....  54.8 us
    pallas_call x1, Pallas kernels, handed_on(): pl.pallas_call(body, out_shape=jax.ShapeDtypeStruct(result.shape, result....  1.83 us

profile of v4, /device:TPU:0, one launch (start us, length us, event | category | flops | bytes accessed | tf_op | source)
XLA Modules:
  0.0 57.9 jit_solution(227821068802692389)
XLA Ops:
  0.0 0.0 copy-start.82
  0.0 0.0 copy-start.85
  0.0 0.0 copy-start.114
  0.0 0.0 copy-start.131
  0.0 0.0 copy-start.134
  0.0 0.0 copy-start.135
  0.0 0.0 copy-start.136
  0.0 54.8 %coupled.1 = (f32[8,64,256]{2,1,0:T(8,128)}, s32[1]{0:T(128)}) custom-call(f32[8,64,256]{2,1,0:T(8,128)} %forcing_hbm.1, f32[8,64,256]{2,1,0:T(8,128)} %thermal_hbm.1, f32[8,64,256]{2,1,0:T(8,128)} %storage_hbm.1, f32[3,8,64,256]{3,2,1,0:T(8,128)} %opening_hbm.1, f32[3,8,64,256]{3,2,1,0:T(8,128)} %flow_hbm.1, f32[8,64,256]{2,1,0:T(8,128)} %root_hbm.1, ...), custom_call_target="tpu_custom_call" | custom-call | tf_op jit(solution)/shard_map/coupled/pallas_call | solution.py:1168
  55.5 0.0 copy-done.82
  55.5 0.0 copy-done.85
  55.6 0.0 copy-done.114
  55.6 0.0 copy-done.131
  55.6 0.0 copy-done.134
  55.6 0.0 copy-done.135
  55.6 0.0 copy-done.136
  55.6 2.0 %conditional.9 = (f32[8,64,256]{2,1,0:T(8,128)}) conditional(s32[]{:T(128)} %bitcast.271, (f32[8,64,256]{2,1,0:T(8,128)}, s32[4,128]{1,0:T(4,128)S(1)}, s32[4,128]{1,0:T(4,128)S(1)}, s32[4,128]{1,0:T(4,128)S(1)}, f32[8,64,256]{2,1,0:T(8,128)}, /*index=5*/f32[4,128]{1,0:T(4,128)S(1)}, f32[3,8,64,256]{3,2,1,0:T(8,128)S(1)}, ...), branch_computations={%region_0.116_spmd, %region_116.117_spmd} | conditional | flops 1876583936 | bytes 522460992 | solution.py:1177
  55.8 1.8 %handed_on.1 = f32[8,64,256]{2,1,0:T(8,128)} custom-call(f32[8,64,256]{2,1,0:T(8,128)} %source), custom_call_target="tpu_custom_call" | custom-call | tf_op jit(solution)/shard_map/cond/branch_1_fun/handed_on/pallas_call | solution.py:1110
Async XLA Ops:
  0.0 55.5 %copy-start.82 = (f32[3,8,64,256]{3,2,1,0:T(8,128)S(1)}, f32[3,8,64,256]{3,2,1,0:T(8,128)}, u32[]{:S(2)}) copy-start(f32[3,8,64,256]{3,2,1,0:T(8,128)} %opening_hbm.1) | copy-start | bytes 4718596
  0.0 55.5 %copy-start.85 = (f32[8,64,256]{2,1,0:T(8,128)S(1)}, f32[8,64,256]{2,1,0:T(8,128)}, u32[]{:S(2)}) copy-start(f32[8,64,256]{2,1,0:T(8,128)} %weight_hbm.1) | copy-start | bytes 1572868
  0.0 55.5 %copy-start.114 = (f32[3,8,8]{2,1,0:T(8,128)S(1)}, f32[3,8,8]{2,1,0:T(8,128)}, u32[]{:S(2)}) copy-start(f32[3,8,8]{2,1,0:T(8,128)} %rigidity_hbm.1) | copy-start | bytes 2308
  0.0 55.6 %copy-start.131 = (f32[4,128]{1,0:T(4,128)S(1)}, f32[4,128]{1,0:T(4,128)}, u32[]{:S(2)}) copy-start(f32[4,128]{1,0:T(4,128)} %factor_hbm.1) | copy-start | bytes 6148
  0.0 55.6 %copy-start.134 = (s32[4,128]{1,0:T(4,128)S(1)}, s32[4,128]{1,0:T(4,128)}, u32[]{:S(2)}) copy-start(s32[4,128]{1,0:T(4,128)} %volume_hbm.1) | copy-start | bytes 6148
  0.0 55.6 %copy-start.135 = (s32[4,128]{1,0:T(4,128)S(1)}, s32[4,128]{1,0:T(4,128)}, u32[]{:S(2)}) copy-start(s32[4,128]{1,0:T(4,128)} %vertex_hbm.1) | copy-start | bytes 6148
  0.0 55.6 %copy-start.136 = (s32[4,128]{1,0:T(4,128)S(1)}, s32[4,128]{1,0:T(4,128)}, u32[]{:S(2)}) copy-start(s32[4,128]{1,0:T(4,128)} %part_hbm.1) | copy-start | bytes 6148

commit v5 on v4

--- a/solution.py
+++ b/solution.py
@@ -225,12 +225,13 @@
 F32 = jnp.float32
 BF16 = jnp.bfloat16
 MESH = pl.DeviceIdType.MESH
-PIVOT_LEAST = 1e-3
-REFINE_MOST = 3e-4
+PIVOT_LEAST = 1e-4
+REFINE_MOST = 4e-3
 PARTS = 4
+SIDE = ITERS + 1
 RAW = {1: ITERS + 1, 2: ITERS + 2}
-DEEP = (3, 5)
-SKIP = tuple(k + 1 for k in DEEP)
+DEEP = (0, 1, 2, 4, 6)
+SKIP = (3, 5, 7)
 
 
 def iota(shape, dim):
@@ -270,9 +271,13 @@
     return jnp.where(lane < ITERS, out, 0.0)
 
 
-def projected(gram, gamma, fluid):
-    shape = gram.shape
+def projected(flat, gamma, fluid):
+    shape = (16, 128)
     row, lane = iota(shape, 0), iota(shape, 1)
+    gram = jnp.zeros(shape, F32)
+    for i in range(SIDE):
+        line = flat if i == 0 else pltpu.roll(flat, 128 - SIDE * i, 1)
+        gram = jnp.where((row == i) & (lane < SIDE), line, gram)
     wide = shift_lanes(gram, gamma)
     if fluid:
         normal, right = shift_rows(wide, gamma), shift_rows(gram, gamma)
@@ -323,7 +328,7 @@
     volume_hbm,
     vertex_hbm,
     factor_hbm,
-    out_hbm,
+    out,
     flag,
     thermal,
     forcing,
@@ -360,12 +365,10 @@
     gram_tile,
     near_slots,
     far_slots,
-    out,
     second,
     ghost,
     ghost_diag,
     load_sem,
-    store_sem,
     halo_send,
     halo_recv,
     coef_send,
@@ -554,9 +557,9 @@
     y_at, z_at = iota(plane, 0), iota(plane, 1)
 
     def write_stats(d_max, d_min, o_sum):
-        lane = iota((8, 128), 1)
+        lane = iota((1, 128), 1)
         tile = jnp.where(lane == 0, greatest(d_max), jnp.where(lane == 1, greatest(-d_min), jnp.where(lane == 2, total(o_sum), 0.0)))
-        near_slots[0, low_id, 0:8] = tile
+        near_slots[0, low_id] = tile
 
     start = (jnp.full((8, depth), -1e30, F32), jnp.full((8, depth), 1e30, F32), jnp.zeros((8, depth), F32))
 
@@ -648,22 +651,22 @@
 
         write_stats(*lax.fori_loop(0, rows, second, start))
 
-    def near_start(which, height):
+    def near_start(which):
         for o, (peer, where) in enumerate(near_peers):
             pltpu.make_async_remote_copy(
-                near_slots.at[which, low_id, pl.ds(0, height)],
-                near_slots.at[which, low_id, pl.ds(0, height)],
+                near_slots.at[which, low_id],
+                near_slots.at[which, low_id],
                 near_send.at[which, o],
                 near_recv.at[which, low_id],
                 device_id=where,
                 device_id_type=MESH,
             ).start()
 
-    def near_wait(which, height):
+    def near_wait(which):
         for o, (peer, where) in enumerate(near_peers):
             copy = pltpu.make_async_remote_copy(
-                near_slots.at[which, peer, pl.ds(0, height)],
-                near_slots.at[which, peer, pl.ds(0, height)],
+                near_slots.at[which, peer],
+                near_slots.at[which, peer],
                 near_send.at[which, o],
                 near_recv.at[which, peer],
                 device_id=where,
@@ -672,22 +675,22 @@
             copy.wait_recv()
             copy.wait_send()
 
-    def far_start(which, height):
+    def far_start(which):
         for o, (peer, where) in enumerate(far_peers):
             pltpu.make_async_remote_copy(
-                far_slots.at[which, high_id, pl.ds(0, height)],
-                far_slots.at[which, high_id, pl.ds(0, height)],
+                far_slots.at[which, high_id],
+                far_slots.at[which, high_id],
                 far_send.at[which, o],
                 far_recv.at[which, high_id],
                 device_id=where,
                 device_id_type=MESH,
             ).start()
 
-    def far_wait(which, height):
+    def far_wait(which):
         for o, (peer, where) in enumerate(far_peers):
             copy = pltpu.make_async_remote_copy(
-                far_slots.at[which, peer, pl.ds(0, height)],
-                far_slots.at[which, peer, pl.ds(0, height)],
+                far_slots.at[which, peer],
+                far_slots.at[which, peer],
                 far_send.at[which, o],
                 far_recv.at[which, peer],
                 device_id=where,
@@ -697,13 +700,13 @@
             copy.wait_send()
 
     def merge_stats(tiles):
-        lane = iota((8, 128), 1)
+        lane = iota((1, 128), 1)
         most, summed = tiles[0], tiles[0]
         for tile in tiles[1:]:
             most, summed = jnp.maximum(most, tile), summed + tile
         return jnp.where(lane == 2, summed, most)
 
-    near_start(0, 8)
+    near_start(0)
 
     l_forcing.wait()
 
@@ -751,12 +754,12 @@
 
     def deep_up(i):
         return pltpu.make_async_remote_copy(
-            basis.at[DEEP[i], rows - 1], second.at[0, i], deep_send.at[i, 0], deep_recv.at[i, 0], device_id=up, device_id_type=MESH
+            basis.at[RAW.get(DEEP[i], DEEP[i]), rows - 1], second.at[0, i], deep_send.at[i, 0], deep_recv.at[i, 0], device_id=up, device_id_type=MESH
         )
 
     def deep_down(i):
         return pltpu.make_async_remote_copy(
-            basis.at[DEEP[i], 2], second.at[1, i], deep_send.at[i, 1], deep_recv.at[i, 1], device_id=down, device_id_type=MESH
+            basis.at[RAW.get(DEEP[i], DEEP[i]), 2], second.at[1, i], deep_send.at[i, 1], deep_recv.at[i, 1], device_id=down, device_id_type=MESH
         )
 
     def ghost_up(i):
@@ -799,6 +802,7 @@
     basis[0, 1 : rows + 1] = forcing[...] + extra
     for j in range(PARTS):
         send_halos(0, j)
+    send_deep(0)
 
     @pl.when(at_bottom)
     def _():
@@ -838,10 +842,10 @@
             return tuple(accs)
 
         accs = lax.fori_loop(0, rows, body, tuple(jnp.zeros((8, depth), F32) for _ in range(k + 1)))
-        row, lane = iota((16, 128), 0), iota((16, 128), 1)
-        tile = jnp.zeros((16, 128), F32) if k == 0 else gram_tile[...]
+        lane = iota((1, 128), 1)
+        tile = jnp.zeros((1, 128), F32) if k == 0 else gram_tile[...]
         for i in range(k + 1):
-            spot = ((row == i) & (lane == k)) | ((row == k) & (lane == i))
+            spot = (lane == i * SIDE + k) | (lane == k * SIDE + i)
             tile = jnp.where(spot, total(accs[i]), tile)
         gram_tile[...] = tile
 
@@ -921,40 +925,49 @@
 
     def extend(i):
         k = DEEP[i]
+        fresh = range(i + 1) if k == 2 else (i,)
 
         def row(side, near, halo, inward):
             v = basis[k, halo]
+            if k == 2:
+                outer_row = mix[0] * second[side, 2] + mix[1] * second[side, 1] + mix[2] * second[side, 0]
+                older = (basis[RAW[1], halo] - center * basis[0, halo]) * inv_e
+            else:
+                outer_row, older = second[side, i], basis[k - 1, halo]
             q = (
                 (ghost[side, 0] - center) * v
                 - ghost[side, 1] * pltpu.roll(v, width - 1, 0)
                 - ghost[side, 2] * pltpu.roll(v, 1, 0)
                 - ghost[side, 3] * pltpu.roll(v, depth - 1, 1)
                 - ghost[side, 4] * pltpu.roll(v, 1, 1)
-                - ghost[side, 5] * second[side, i]
+                - ghost[side, 5] * outer_row
                 - inward * basis[k, near]
             )
-            basis[k + 1, halo] = scale * q - basis[k - 1, halo]
+            basis[k + 1, halo] = scale * q - older
 
         @pl.when(far_down)
         def _():
-            deep_up(i).wait_recv()
-            if i == 0:
+            for n in fresh:
+                deep_up(n).wait_recv()
+            if k == 2:
                 for n in range(6):
                     ghost_up(n).wait_recv()
             row(0, 1, 0, ax[0])
 
         @pl.when(far_up)
         def _():
-            deep_down(i).wait_recv()
-            if i == 0:
+            for n in fresh:
+                deep_down(n).wait_recv()
+            if k == 2:
                 for n in range(6):
                     ghost_down(n).wait_recv()
             row(1, rows, rows + 1, gx[rows])
 
     apply(0, None)
-    near_wait(0, 8)
-    far_slots[0, high_id, 0:8] = merge_stats([near_slots[0, i, 0:8] for i in range(inner)])
-    far_start(0, 8)
+    send_deep(1)
+    near_wait(0)
+    far_slots[0, high_id] = merge_stats([near_slots[0, i] for i in range(inner)])
+    far_start(0)
     finish(0, None)
 
     @pl.when(far_up)
@@ -970,20 +983,21 @@
             ghost_down(n).start()
 
     apply(1, None)
+    send_deep(2)
     gram_row(0)
     finish(1, None)
-    far_wait(0, 8)
+    far_wait(0)
     split = (groups - 1) * outer
 
-    def interval(tiles, count):
+    def interval(tiles, count, of_most, of_mean):
         stats = merge_stats(tiles)
         mean = stats[0:1, 2:3] * (1.0 / count)
-        high = stats[0:1, 0:1] + 0.25 * mean
+        high = of_most * stats[0:1, 0:1] + of_mean * mean
         low = jnp.maximum(-stats[0:1, 1:2] - 0.5 * mean, 0.0)
         return 0.5 * (high + low), 0.5 * (high - low)
 
-    c_fluid, e_fluid = interval([far_slots[0, i, 0:8] for i in range(split)], float((groups - 1) * bricks * cells * depth))
-    c_solid, e_solid = interval([far_slots[0, i, 0:8] for i in range(split, n_far)], float(bricks * cells * depth))
+    c_fluid, e_fluid = interval([far_slots[0, i] for i in range(split)], float((groups - 1) * bricks * cells * depth), 0.9, 0.1)
+    c_solid, e_solid = interval([far_slots[0, i] for i in range(split, n_far)], float(bricks * cells * depth), 0.97, 0.25)
     center = jnp.where(solid, c_solid, c_fluid)
     inv_e = 1.0 / jnp.where(solid, e_solid, e_fluid)
     scale = 2.0 * inv_e
@@ -1006,19 +1020,19 @@
             gram_row(1)
         gram_row(k)
         finish(k, scale, mix if k == 2 else None)
-        if k in DEEP:
+        if k + 1 in SKIP:
             extend(DEEP.index(k))
     gram_row(ITERS)
 
     near_slots[1, low_id] = gram_tile[...]
-    near_start(1, 16)
-    near_wait(1, 16)
+    near_start(1)
+    near_wait(1)
     summed = near_slots[1, 0]
     for i in range(1, inner):
         summed = summed + near_slots[1, i]
     far_slots[1, high_id] = summed
-    far_start(1, 16)
-    far_wait(1, 16)
+    far_start(1)
+    far_wait(1)
     gram_fluid = far_slots[1, 0]
     for i in range(1, split):
         gram_fluid = gram_fluid + far_slots[1, i]
@@ -1036,7 +1050,6 @@
         for k in range(1, ITERS):
             acc = acc + weights[k] * basis[k, r + 1]
         out[r] = acc
-        pltpu.make_async_copy(out.at[r], out_hbm.at[r], store_sem.at[r]).start()
         return carry
 
     lax.fori_loop(0, rows, combine, 0)
@@ -1089,32 +1102,21 @@
             def _():
                 halo_down(k, j).wait_send()
 
-    for r in range(rows):
-        pltpu.make_async_copy(out.at[r], out_hbm.at[r], store_sem.at[r]).wait()
-
 
 def handed_on(result):
-    rows = result.shape[0]
-
-    def body(source, target, held, in_sem, out_sem):
-        ins = [pltpu.make_async_copy(source.at[i], held.at[i], in_sem.at[i]) for i in range(rows)]
-        outs = [pltpu.make_async_copy(held.at[i], target.at[i], out_sem.at[i]) for i in range(rows)]
-        for copy in ins:
-            copy.start()
-        for arrived, copy in zip(ins, outs):
-            arrived.wait()
-            copy.start()
-        for copy in outs:
-            copy.wait()
+    def body(source, target, sem):
+        copy = pltpu.make_async_copy(source, target, sem)
+        copy.start()
+        copy.wait()
 
     return pl.pallas_call(
         body,
         out_shape=jax.ShapeDtypeStruct(result.shape, result.dtype),
-        in_specs=[pl.BlockSpec(memory_space=pl.ANY)],
+        in_specs=[pl.BlockSpec(memory_space=pltpu.VMEM)],
         out_specs=pl.BlockSpec(memory_space=pl.ANY),
-        scratch_shapes=[pltpu.VMEM(result.shape, F32), pltpu.SemaphoreType.DMA((rows,)), pltpu.SemaphoreType.DMA((rows,))],
+        scratch_shapes=[pltpu.SemaphoreType.DMA],
         name="handed_on",
-    )(result)
+    )(pltpu.with_memory_space_constraint(result, pltpu.VMEM))
 
 
 def shards(*arguments):
@@ -1142,14 +1144,12 @@
         + [vm((rows * width, points), BF16), vm((depth, points), BF16)]
         + [vm((8, 128), F32)] * 2
         + [vm((groups - 1, 8, 128), F32)]
-        + [vm((16, 128), F32), vm((2, 8, 16, 128), F32), vm((2, n_far, 16, 128), F32)]
-        + [vm(slab, F32)]
+        + [vm((1, 128), F32), vm((2, 8, 1, 128), F32), vm((2, n_far, 1, 128), F32)]
         + [vm((2, len(DEEP), width, depth), F32), vm((2, 6, width, depth), F32), vm((2, width, depth), F32)]
     )
     dma = pltpu.SemaphoreType.DMA
     semaphores = [
         dma((12,)),
-        dma((rows,)),
         dma((ITERS, 2, PARTS)),
         dma((ITERS, 2, PARTS)),
         dma((2,)),
@@ -1167,9 +1167,9 @@
     ]
     result, flag = pl.pallas_call(
         functools.partial(kernel, groups, bricks),
-        out_shape=(jax.ShapeDtypeStruct(slab, F32), jax.ShapeDtypeStruct((1,), jnp.int32)),
+        out_shape=(pltpu.VMEM(slab, F32), jax.ShapeDtypeStruct((1,), jnp.int32)),
         in_specs=[pl.BlockSpec(memory_space=pl.ANY)] * 12,
-        out_specs=(pl.BlockSpec(memory_space=pl.ANY), pl.BlockSpec(memory_space=pltpu.SMEM)),
+        out_specs=(pl.BlockSpec(memory_space=pltpu.VMEM), pl.BlockSpec(memory_space=pltpu.SMEM)),
         scratch_shapes=scratch + semaphores,
         compiler_params=pltpu.CompilerParams(collective_id=0, has_side_effects=True, vmem_limit_bytes=56 * 2**20),
         name="coupled",

time: 58.1 us -> 54.4 us (0.936)
  Pallas kernels: 56.6 us -> 53 us
    pallas_call x1, Pallas kernels: 54.8 us -> 52.2 us  [shards(): pl.pallas_call(functools.partial(kernel, groups, bricks), out_shape=(pltp...]
    pallas_call x1, Pallas kernels: 1.83 us -> 0.8 us  [handed_on(): pl.pallas_call(body, out_shape=jax.ShapeDtypeStruct(result.shape, result....]
where the time goes in v5:
time: 54.4 us; the launch traced here: 54.3 us
  Pallas kernels  53 us (97%)
  between operations  0.97 us (2%)
    pallas_call x1, Pallas kernels, shards(): pl.pallas_call(functools.partial(kernel, groups, bricks), out_shape=(pltp...  52.2 us

profile of v5, /device:TPU:0, one launch (start us, length us, event | category | flops | bytes accessed | tf_op | source)
XLA Modules:
  0.0 54.3 jit_solution(10157812064784710783)
XLA Ops:
  0.0 0.0 copy-start.82
  0.0 0.0 copy-start.85
  0.0 0.0 copy-start.102
  0.0 0.0 copy-start.113
  0.0 0.0 copy-start.130
  0.0 0.0 copy-start.133
  0.0 0.0 copy-start.134
  0.0 0.0 copy-start.135
  0.0 52.2 %coupled.1 = (f32[8,64,256]{2,1,0:T(8,128)S(1)}, s32[1]{0:T(128)}) custom-call(f32[8,64,256]{2,1,0:T(8,128)} %forcing_hbm.1, f32[8,64,256]{2,1,0:T(8,128)} %thermal_hbm.1, f32[8,64,256]{2,1,0:T(8,128)} %storage_hbm.1, f32[3,8,64,256]{3,2,1,0:T(8,128)} %opening_hbm.1, f32[3,8,64,256]{3,2,1,0:T(8,128)} %flow_hbm.1, f32[8,64,256]{2,1,0:T(8,128)} %root_hbm.1, ...), custom_call_target="tpu_custom_call" | custom-call | tf_op jit(solution)/shard_map/coupled/pallas_call | solution.py:1168
  53.0 0.0 copy-done.82
  53.0 0.0 copy-done.85
  53.0 0.0 copy-done.102
  53.0 0.0 copy-done.113
  53.0 0.0 copy-done.130
  53.0 0.0 copy-done.133
  53.0 0.0 copy-done.134
  53.0 0.0 copy-done.135
  53.0 1.0 %conditional.9 = (f32[8,64,256]{2,1,0:T(8,128)}) conditional(s32[]{:T(128)} %bitcast.271, (f32[8,64,256]{2,1,0:T(8,128)}, s32[4,128]{1,0:T(4,128)S(1)}, s32[4,128]{1,0:T(4,128)S(1)}, s32[4,128]{1,0:T(4,128)S(1)}, f32[8,64,256]{2,1,0:T(8,128)S(1)}, /*index=5*/f32[4,128]{1,0:T(4,128)S(1)}, f32[3,8,64,256]{3,2,1,0:T(8,128)S(1)}, ...), branch_computations={%region_0.116_spmd, %region_116.117_spmd} | conditional | flops 1876583936 | bytes 517717760 | solution.py:1177
  53.3 0.8 %handed_on.1 = f32[8,64,256]{2,1,0:T(8,128)} custom-call(f32[8,64,256]{2,1,0:T(8,128)S(1)} %source), custom_call_target="tpu_custom_call" | custom-call | tf_op jit(solution)/shard_map/cond/branch_1_fun/handed_on/pallas_call | solution.py:1112
Async XLA Ops:
  0.0 53.0 %copy-start.82 = (f32[3,8,64,256]{3,2,1,0:T(8,128)S(1)}, f32[3,8,64,256]{3,2,1,0:T(8,128)}, u32[]{:S(2)}) copy-start(f32[3,8,64,256]{3,2,1,0:T(8,128)} %opening_hbm.1) | copy-start | bytes 4718596
  0.0 53.0 %copy-start.85 = (f32[8,64,256]{2,1,0:T(8,128)S(1)}, f32[8,64,256]{2,1,0:T(8,128)}, u32[]{:S(2)}) copy-start(f32[8,64,256]{2,1,0:T(8,128)} %weight_hbm.1) | copy-start | bytes 1572868
  0.0 53.0 %copy-start.102 = (f32[8,64,256]{2,1,0:T(8,128)S(1)}, f32[8,64,256]{2,1,0:T(8,128)}, u32[]{:S(2)}) copy-start(f32[8,64,256]{2,1,0:T(8,128)} %thermal_hbm.1) | copy-start | bytes 1572868
  0.0 53.0 %copy-start.113 = (f32[3,8,8]{2,1,0:T(8,128)S(1)}, f32[3,8,8]{2,1,0:T(8,128)}, u32[]{:S(2)}) copy-start(f32[3,8,8]{2,1,0:T(8,128)} %rigidity_hbm.1) | copy-start | bytes 2308
  0.0 53.0 %copy-start.130 = (f32[4,128]{1,0:T(4,128)S(1)}, f32[4,128]{1,0:T(4,128)}, u32[]{:S(2)}) copy-start(f32[4,128]{1,0:T(4,128)} %factor_hbm.1) | copy-start | bytes 6148
  0.0 53.0 %copy-start.133 = (s32[4,128]{1,0:T(4,128)S(1)}, s32[4,128]{1,0:T(4,128)}, u32[]{:S(2)}) copy-start(s32[4,128]{1,0:T(4,128)} %volume_hbm.1) | copy-start | bytes 6148
  0.0 53.0 %copy-start.134 = (s32[4,128]{1,0:T(4,128)S(1)}, s32[4,128]{1,0:T(4,128)}, u32[]{:S(2)}) copy-start(s32[4,128]{1,0:T(4,128)} %vertex_hbm.1) | copy-start | bytes 6148
  0.0 53.0 %copy-start.135 = (s32[4,128]{1,0:T(4,128)S(1)}, s32[4,128]{1,0:T(4,128)}, u32[]{:S(2)}) copy-start(s32[4,128]{1,0:T(4,128)} %part_hbm.1) | copy-start | bytes 6148

commit v6 on v5

--- a/solution.py
+++ b/solution.py
@@ -830,7 +830,7 @@
     def _():
         ax[rows] = jnp.zeros(plane, F32)
 
-    def gram_row(k):
+    def gram_sums(k, low, high, accs):
         def body(r, accs):
             accs = list(accs)
             for j in range(width // 8):
@@ -841,13 +841,21 @@
                     accs[i] = accs[i] + mine * other
             return tuple(accs)
 
-        accs = lax.fori_loop(0, rows, body, tuple(jnp.zeros((8, depth), F32) for _ in range(k + 1)))
+        return lax.fori_loop(low, high, body, accs)
+
+    def gram_none(k):
+        return tuple(jnp.zeros((8, depth), F32) for _ in range(k + 1))
+
+    def gram_keep(k, accs):
         lane = iota((1, 128), 1)
         tile = jnp.zeros((1, 128), F32) if k == 0 else gram_tile[...]
         for i in range(k + 1):
             spot = (lane == i * SIDE + k) | (lane == k * SIDE + i)
             tile = jnp.where(spot, total(accs[i]), tile)
         gram_tile[...] = tile
+
+    def gram_row(k):
+        gram_keep(k, gram_sums(k, 0, rows, gram_none(k)))
 
     def local(r, v):
         return (
@@ -1019,10 +1027,13 @@
         if k == 2:
             gram_row(1)
         gram_row(k)
+        if k + 1 == ITERS:
+            last_sums = gram_sums(ITERS, 1, rows - 1, gram_none(ITERS))
         finish(k, scale, mix if k == 2 else None)
         if k + 1 in SKIP:
             extend(DEEP.index(k))
-    gram_row(ITERS)
+    last_sums = gram_sums(ITERS, rows - 1, rows, gram_sums(ITERS, 0, 1, last_sums))
+    gram_keep(ITERS, last_sums)
 
     near_slots[1, low_id] = gram_tile[...]
     near_start(1)
@@ -1032,6 +1043,55 @@
         summed = summed + near_slots[1, i]
     far_slots[1, high_id] = summed
     far_start(1)
+
+    @pl.when(solid)
+    def _():
+        for g in range(groups - 1):
+            wall_copy(g).wait_send()
+
+    @pl.when(fluid)
+    def _():
+        near_copy.wait_send()
+
+    @pl.when(fluid & has_up)
+    def _():
+        coef_a.wait_send()
+        coef_g.wait_send()
+
+    @pl.when(solid & has_up)
+    def _():
+        coef_up.wait_send()
+
+    @pl.when(solid & has_down)
+    def _():
+        coef_down.wait_send()
+
+    @pl.when(far_up)
+    def _():
+        for n in range(6):
+            ghost_up(n).wait_send()
+        for i in range(len(DEEP)):
+            deep_up(i).wait_send()
+
+    @pl.when(far_down)
+    def _():
+        for n in range(6):
+            ghost_down(n).wait_send()
+        for i in range(len(DEEP)):
+            deep_down(i).wait_send()
+
+    for k in range(ITERS):
+        sent_up, sent_down = linked(k)
+        for j in range(PARTS):
+
+            @pl.when(sent_up)
+            def _():
+                halo_up(k, j).wait_send()
+
+            @pl.when(sent_down)
+            def _():
+                halo_down(k, j).wait_send()
+
     far_wait(1)
     gram_fluid = far_slots[1, 0]
     for i in range(1, split):
@@ -1053,54 +1113,6 @@
         return carry
 
     lax.fori_loop(0, rows, combine, 0)
-
-    @pl.when(solid)
-    def _():
-        for g in range(groups - 1):
-            wall_copy(g).wait_send()
-
-    @pl.when(fluid)
-    def _():
-        near_copy.wait_send()
-
-    @pl.when(fluid & has_up)
-    def _():
-        coef_a.wait_send()
-        coef_g.wait_send()
-
-    @pl.when(solid & has_up)
-    def _():
-        coef_up.wait_send()
-
-    @pl.when(solid & has_down)
-    def _():
-        coef_down.wait_send()
-
-    @pl.when(far_up)
-    def _():
-        for n in range(6):
-            ghost_up(n).wait_send()
-        for i in range(len(DEEP)):
-            deep_up(i).wait_send()
-
-    @pl.when(far_down)
-    def _():
-        for n in range(6):
-            ghost_down(n).wait_send()
-        for i in range(len(DEEP)):
-            deep_down(i).wait_send()
-
-    for k in range(ITERS):
-        sent_up, sent_down = linked(k)
-        for j in range(PARTS):
-
-            @pl.when(sent_up)
-            def _():
-                halo_up(k, j).wait_send()
-
-            @pl.when(sent_down)
-            def _():
-                halo_down(k, j).wait_send()
 
 
 def handed_on(result):

time: 54.4 us -> 53.9 us (level)
  no operation moved by 1% of the time
where the time goes in v6:
time: 53.9 us; the launch traced here: 53.8 us
  Pallas kernels  52.5 us (97%)
  between operations  0.97 us (2%)
    pallas_call x1, Pallas kernels, shards(): pl.pallas_call(functools.partial(kernel, groups, bricks), out_shape=(pltp...  51.7 us

profile of v6, /device:TPU:0, one launch (start us, length us, event | category | flops | bytes accessed | tf_op | source)
XLA Modules:
  0.0 53.8 jit_solution(6534556472776451993)
XLA Ops:
  0.0 0.0 copy-start.82
  0.0 0.0 copy-start.85
  0.0 0.0 copy-start.102
  0.0 0.0 copy-start.113
  0.0 0.0 copy-start.130
  0.0 0.0 copy-start.133
  0.0 0.0 copy-start.134
  0.0 0.0 copy-start.135
  0.0 51.7 %coupled.1 = (f32[8,64,256]{2,1,0:T(8,128)S(1)}, s32[1]{0:T(128)}) custom-call(f32[8,64,256]{2,1,0:T(8,128)} %forcing_hbm.1, f32[8,64,256]{2,1,0:T(8,128)} %thermal_hbm.1, f32[8,64,256]{2,1,0:T(8,128)} %storage_hbm.1, f32[3,8,64,256]{3,2,1,0:T(8,128)} %opening_hbm.1, f32[3,8,64,256]{3,2,1,0:T(8,128)} %flow_hbm.1, f32[8,64,256]{2,1,0:T(8,128)} %root_hbm.1, ...), custom_call_target="tpu_custom_call" | custom-call | tf_op jit(solution)/shard_map/coupled/pallas_call | solution.py:1180
  52.5 0.0 copy-done.82
  52.5 0.0 copy-done.85
  52.5 0.0 copy-done.102
  52.5 0.0 copy-done.113
  52.5 0.0 copy-done.130
  52.5 0.0 copy-done.133
  52.5 0.0 copy-done.134
  52.5 0.0 copy-done.135
  52.5 1.0 %conditional.9 = (f32[8,64,256]{2,1,0:T(8,128)}) conditional(s32[]{:T(128)} %bitcast.271, (f32[8,64,256]{2,1,0:T(8,128)}, s32[4,128]{1,0:T(4,128)S(1)}, s32[4,128]{1,0:T(4,128)S(1)}, s32[4,128]{1,0:T(4,128)S(1)}, f32[8,64,256]{2,1,0:T(8,128)S(1)}, /*index=5*/f32[4,128]{1,0:T(4,128)S(1)}, f32[3,8,64,256]{3,2,1,0:T(8,128)S(1)}, ...), branch_computations={%region_0.116_spmd, %region_116.117_spmd} | conditional | flops 1876583936 | bytes 517717760 | solution.py:1189
  52.8 0.8 %handed_on.1 = f32[8,64,256]{2,1,0:T(8,128)} custom-call(f32[8,64,256]{2,1,0:T(8,128)S(1)} %source), custom_call_target="tpu_custom_call" | custom-call | tf_op jit(solution)/shard_map/cond/branch_1_fun/handed_on/pallas_call | solution.py:1124
Async XLA Ops:
  0.0 52.5 %copy-start.82 = (f32[3,8,64,256]{3,2,1,0:T(8,128)S(1)}, f32[3,8,64,256]{3,2,1,0:T(8,128)}, u32[]{:S(2)}) copy-start(f32[3,8,64,256]{3,2,1,0:T(8,128)} %opening_hbm.1) | copy-start | bytes 4718596
  0.0 52.5 %copy-start.85 = (f32[8,64,256]{2,1,0:T(8,128)S(1)}, f32[8,64,256]{2,1,0:T(8,128)}, u32[]{:S(2)}) copy-start(f32[8,64,256]{2,1,0:T(8,128)} %weight_hbm.1) | copy-start | bytes 1572868
  0.0 52.5 %copy-start.102 = (f32[8,64,256]{2,1,0:T(8,128)S(1)}, f32[8,64,256]{2,1,0:T(8,128)}, u32[]{:S(2)}) copy-start(f32[8,64,256]{2,1,0:T(8,128)} %thermal_hbm.1) | copy-start | bytes 1572868
  0.0 52.5 %copy-start.113 = (f32[3,8,8]{2,1,0:T(8,128)S(1)}, f32[3,8,8]{2,1,0:T(8,128)}, u32[]{:S(2)}) copy-start(f32[3,8,8]{2,1,0:T(8,128)} %rigidity_hbm.1) | copy-start | bytes 2308
  0.0 52.5 %copy-start.130 = (f32[4,128]{1,0:T(4,128)S(1)}, f32[4,128]{1,0:T(4,128)}, u32[]{:S(2)}) copy-start(f32[4,128]{1,0:T(4,128)} %factor_hbm.1) | copy-start | bytes 6148
  0.0 52.5 %copy-start.133 = (s32[4,128]{1,0:T(4,128)S(1)}, s32[4,128]{1,0:T(4,128)}, u32[]{:S(2)}) copy-start(s32[4,128]{1,0:T(4,128)} %volume_hbm.1) | copy-start | bytes 6148
  0.0 52.5 %copy-start.134 = (s32[4,128]{1,0:T(4,128)S(1)}, s32[4,128]{1,0:T(4,128)}, u32[]{:S(2)}) copy-start(s32[4,128]{1,0:T(4,128)} %vertex_hbm.1) | copy-start | bytes 6148
  0.0 52.5 %copy-start.135 = (s32[4,128]{1,0:T(4,128)S(1)}, s32[4,128]{1,0:T(4,128)}, u32[]{:S(2)}) copy-start(s32[4,128]{1,0:T(4,128)} %part_hbm.1) | copy-start | bytes 6148

commit v7 on v6

--- a/solution.py
+++ b/solution.py
@@ -421,7 +421,7 @@
         (forcing_hbm, forcing),
     ]
     loads = [pltpu.make_async_copy(s, d, load_sem.at[i]) for i, (s, d) in enumerate(names)]
-    for load in loads:
+    for load in loads[:3]:
         load.start()
     (l_vertex, l_volume, l_thermal, l_part, l_factor, l_opening, l_flow, l_storage, l_weight, l_root, l_rigid, l_forcing) = loads
 
@@ -450,6 +450,9 @@
     @pl.when(has_down)
     def _():
         pl.semaphore_signal(barrier, inc=1, device_id=down, device_id_type=MESH)
+
+    for load in loads[3:]:
+        load.start()
 
     @pl.when(at_bottom)
     def _():

time: 53.9 us -> 53.9 us (level)
  no operation moved by 1% of the time
where the time goes in v7:
time: 53.9 us; the launch traced here: 53.8 us
  Pallas kernels  52.5 us (97%)
  between operations  0.97 us (2%)
    pallas_call x1, Pallas kernels, shards(): pl.pallas_call(functools.partial(kernel, groups, bricks), out_shape=(pltp...  51.7 us

profile of v7, /device:TPU:0, one launch (start us, length us, event | category | flops | bytes accessed | tf_op | source)
XLA Modules:
  0.0 53.8 jit_solution(11849872920089137170)
XLA Ops:
  0.0 0.0 copy-start.82
  0.0 0.0 copy-start.85
  0.0 0.0 copy-start.102
  0.0 0.0 copy-start.113
  0.0 0.0 copy-start.130
  0.0 0.0 copy-start.133
  0.0 0.0 copy-start.134
  0.0 0.0 copy-start.135
  0.0 51.7 %coupled.1 = (f32[8,64,256]{2,1,0:T(8,128)S(1)}, s32[1]{0:T(128)}) custom-call(f32[8,64,256]{2,1,0:T(8,128)} %forcing_hbm.1, f32[8,64,256]{2,1,0:T(8,128)} %thermal_hbm.1, f32[8,64,256]{2,1,0:T(8,128)} %storage_hbm.1, f32[3,8,64,256]{3,2,1,0:T(8,128)} %opening_hbm.1, f32[3,8,64,256]{3,2,1,0:T(8,128)} %flow_hbm.1, f32[8,64,256]{2,1,0:T(8,128)} %root_hbm.1, ...), custom_call_target="tpu_custom_call" | custom-call | tf_op jit(solution)/shard_map/coupled/pallas_call | solution.py:1183
  52.5 0.0 copy-done.82
  52.5 0.0 copy-done.85
  52.5 0.0 copy-done.102
  52.5 0.0 copy-done.113
  52.5 0.0 copy-done.130
  52.5 0.0 copy-done.133
  52.5 0.0 copy-done.134
  52.5 0.0 copy-done.135
  52.5 1.0 %conditional.9 = (f32[8,64,256]{2,1,0:T(8,128)}) conditional(s32[]{:T(128)} %bitcast.271, (f32[8,64,256]{2,1,0:T(8,128)}, s32[4,128]{1,0:T(4,128)S(1)}, s32[4,128]{1,0:T(4,128)S(1)}, s32[4,128]{1,0:T(4,128)S(1)}, f32[8,64,256]{2,1,0:T(8,128)S(1)}, /*index=5*/f32[4,128]{1,0:T(4,128)S(1)}, f32[3,8,64,256]{3,2,1,0:T(8,128)S(1)}, ...), branch_computations={%region_0.116_spmd, %region_116.117_spmd} | conditional | flops 1876583936 | bytes 517717760 | solution.py:1192
  52.8 0.8 %handed_on.1 = f32[8,64,256]{2,1,0:T(8,128)} custom-call(f32[8,64,256]{2,1,0:T(8,128)S(1)} %source), custom_call_target="tpu_custom_call" | custom-call | tf_op jit(solution)/shard_map/cond/branch_1_fun/handed_on/pallas_call | solution.py:1127
Async XLA Ops:
  0.0 52.5 %copy-start.82 = (f32[3,8,64,256]{3,2,1,0:T(8,128)S(1)}, f32[3,8,64,256]{3,2,1,0:T(8,128)}, u32[]{:S(2)}) copy-start(f32[3,8,64,256]{3,2,1,0:T(8,128)} %opening_hbm.1) | copy-start | bytes 4718596
  0.0 52.5 %copy-start.85 = (f32[8,64,256]{2,1,0:T(8,128)S(1)}, f32[8,64,256]{2,1,0:T(8,128)}, u32[]{:S(2)}) copy-start(f32[8,64,256]{2,1,0:T(8,128)} %weight_hbm.1) | copy-start | bytes 1572868
  0.0 52.5 %copy-start.102 = (f32[8,64,256]{2,1,0:T(8,128)S(1)}, f32[8,64,256]{2,1,0:T(8,128)}, u32[]{:S(2)}) copy-start(f32[8,64,256]{2,1,0:T(8,128)} %thermal_hbm.1) | copy-start | bytes 1572868
  0.0 52.5 %copy-start.113 = (f32[3,8,8]{2,1,0:T(8,128)S(1)}, f32[3,8,8]{2,1,0:T(8,128)}, u32[]{:S(2)}) copy-start(f32[3,8,8]{2,1,0:T(8,128)} %rigidity_hbm.1) | copy-start | bytes 2308
  0.0 52.5 %copy-start.130 = (f32[4,128]{1,0:T(4,128)S(1)}, f32[4,128]{1,0:T(4,128)}, u32[]{:S(2)}) copy-start(f32[4,128]{1,0:T(4,128)} %factor_hbm.1) | copy-start | bytes 6148
  0.0 52.5 %copy-start.133 = (s32[4,128]{1,0:T(4,128)S(1)}, s32[4,128]{1,0:T(4,128)}, u32[]{:S(2)}) copy-start(s32[4,128]{1,0:T(4,128)} %volume_hbm.1) | copy-start | bytes 6148
  0.0 52.5 %copy-start.134 = (s32[4,128]{1,0:T(4,128)S(1)}, s32[4,128]{1,0:T(4,128)}, u32[]{:S(2)}) copy-start(s32[4,128]{1,0:T(4,128)} %vertex_hbm.1) | copy-start | bytes 6148
  0.0 52.5 %copy-start.135 = (s32[4,128]{1,0:T(4,128)S(1)}, s32[4,128]{1,0:T(4,128)}, u32[]{:S(2)}) copy-start(s32[4,128]{1,0:T(4,128)} %part_hbm.1) | copy-start | bytes 6148

commit v8 on v7

--- a/solution.py
+++ b/solution.py
@@ -227,7 +227,7 @@
 MESH = pl.DeviceIdType.MESH
 PIVOT_LEAST = 1e-4
 REFINE_MOST = 4e-3
-PARTS = 4
+PARTS = 8
 SIDE = ITERS + 1
 RAW = {1: ITERS + 1, 2: ITERS + 2}
 DEEP = (0, 1, 2, 4, 6)
@@ -676,7 +676,17 @@
                 device_id_type=MESH,
             )
             copy.wait_recv()
-            copy.wait_send()
+
+    def near_sent(which):
+        for o, (peer, where) in enumerate(near_peers):
+            pltpu.make_async_remote_copy(
+                near_slots.at[which, low_id],
+                near_slots.at[which, low_id],
+                near_send.at[which, o],
+                near_recv.at[which, low_id],
+                device_id=where,
+                device_id_type=MESH,
+            ).wait_send()
 
     def far_start(which):
         for o, (peer, where) in enumerate(far_peers):
@@ -1046,6 +1056,8 @@
         summed = summed + near_slots[1, i]
     far_slots[1, high_id] = summed
     far_start(1)
+    near_sent(0)
+    near_sent(1)
 
     @pl.when(solid)
     def _():

time: 53.9 us -> 55 us (1.020)
  Pallas kernels: 52.5 us -> 53.6 us
    pallas_call x1, Pallas kernels: 51.7 us -> 52.8 us  [shards(): pl.pallas_call(functools.partial(kernel, groups, bricks), out_shape=(pltp...]
where the time goes in v8:
time: 55 us; the launch traced here: 54.9 us
  Pallas kernels  53.6 us (97%)
  between operations  0.99 us (2%)
    pallas_call x1, Pallas kernels, shards(): pl.pallas_call(functools.partial(kernel, groups, bricks), out_shape=(pltp...  52.8 us

profile of v8, /device:TPU:0, one launch (start us, length us, event | category | flops | bytes accessed | tf_op | source)
XLA Modules:
  0.0 54.9 jit_solution(17626551773332883198)
XLA Ops:
  0.0 0.0 copy-start.82
  0.0 0.0 copy-start.85
  0.0 0.0 copy-start.102
  0.0 0.0 copy-start.113
  0.0 0.0 copy-start.130
  0.0 0.0 copy-start.133
  0.0 0.0 copy-start.134
  0.0 0.0 copy-start.135
  0.0 52.8 %coupled.1 = (f32[8,64,256]{2,1,0:T(8,128)S(1)}, s32[1]{0:T(128)}) custom-call(f32[8,64,256]{2,1,0:T(8,128)} %forcing_hbm.1, f32[8,64,256]{2,1,0:T(8,128)} %thermal_hbm.1, f32[8,64,256]{2,1,0:T(8,128)} %storage_hbm.1, f32[3,8,64,256]{3,2,1,0:T(8,128)} %opening_hbm.1, f32[3,8,64,256]{3,2,1,0:T(8,128)} %flow_hbm.1, f32[8,64,256]{2,1,0:T(8,128)} %root_hbm.1, ...), custom_call_target="tpu_custom_call" | custom-call | tf_op jit(solution)/shard_map/coupled/pallas_call | solution.py:1195
  53.5 0.0 copy-done.82
  53.5 0.0 copy-done.85
  53.5 0.0 copy-done.102
  53.5 0.0 copy-done.113
  53.5 0.0 copy-done.130
  53.5 0.0 copy-done.133
  53.6 0.0 copy-done.134
  53.6 0.0 copy-done.135
  53.6 1.1 %conditional.9 = (f32[8,64,256]{2,1,0:T(8,128)}) conditional(s32[]{:T(128)} %bitcast.271, (f32[8,64,256]{2,1,0:T(8,128)}, s32[4,128]{1,0:T(4,128)S(1)}, s32[4,128]{1,0:T(4,128)S(1)}, s32[4,128]{1,0:T(4,128)S(1)}, f32[8,64,256]{2,1,0:T(8,128)S(1)}, /*index=5*/f32[4,128]{1,0:T(4,128)S(1)}, f32[3,8,64,256]{3,2,1,0:T(8,128)S(1)}, ...), branch_computations={%region_0.116_spmd, %region_116.117_spmd} | conditional | flops 1876583936 | bytes 517717760 | solution.py:1204
  53.9 0.8 %handed_on.1 = f32[8,64,256]{2,1,0:T(8,128)} custom-call(f32[8,64,256]{2,1,0:T(8,128)S(1)} %source), custom_call_target="tpu_custom_call" | custom-call | tf_op jit(solution)/shard_map/cond/branch_1_fun/handed_on/pallas_call | solution.py:1139
Async XLA Ops:
  0.0 53.5 %copy-start.82 = (f32[3,8,64,256]{3,2,1,0:T(8,128)S(1)}, f32[3,8,64,256]{3,2,1,0:T(8,128)}, u32[]{:S(2)}) copy-start(f32[3,8,64,256]{3,2,1,0:T(8,128)} %opening_hbm.1) | copy-start | bytes 4718596
  0.0 53.5 %copy-start.85 = (f32[8,64,256]{2,1,0:T(8,128)S(1)}, f32[8,64,256]{2,1,0:T(8,128)}, u32[]{:S(2)}) copy-start(f32[8,64,256]{2,1,0:T(8,128)} %weight_hbm.1) | copy-start | bytes 1572868
  0.0 53.5 %copy-start.102 = (f32[8,64,256]{2,1,0:T(8,128)S(1)}, f32[8,64,256]{2,1,0:T(8,128)}, u32[]{:S(2)}) copy-start(f32[8,64,256]{2,1,0:T(8,128)} %thermal_hbm.1) | copy-start | bytes 1572868
  0.0 53.5 %copy-start.113 = (f32[3,8,8]{2,1,0:T(8,128)S(1)}, f32[3,8,8]{2,1,0:T(8,128)}, u32[]{:S(2)}) copy-start(f32[3,8,8]{2,1,0:T(8,128)} %rigidity_hbm.1) | copy-start | bytes 2308
  0.0 53.5 %copy-start.130 = (f32[4,128]{1,0:T(4,128)S(1)}, f32[4,128]{1,0:T(4,128)}, u32[]{:S(2)}) copy-start(f32[4,128]{1,0:T(4,128)} %factor_hbm.1) | copy-start | bytes 6148
  0.0 53.5 %copy-start.133 = (s32[4,128]{1,0:T(4,128)S(1)}, s32[4,128]{1,0:T(4,128)}, u32[]{:S(2)}) copy-start(s32[4,128]{1,0:T(4,128)} %volume_hbm.1) | copy-start | bytes 6148
  0.0 53.5 %copy-start.134 = (s32[4,128]{1,0:T(4,128)S(1)}, s32[4,128]{1,0:T(4,128)}, u32[]{:S(2)}) copy-start(s32[4,128]{1,0:T(4,128)} %vertex_hbm.1) | copy-start | bytes 6148
  0.0 53.5 %copy-start.135 = (s32[4,128]{1,0:T(4,128)S(1)}, s32[4,128]{1,0:T(4,128)}, u32[]{:S(2)}) copy-start(s32[4,128]{1,0:T(4,128)} %part_hbm.1) | copy-start | bytes 6148
